TPU v7x, 512 devices: a whole 4x4x16 slice. The times are simulated.
512 devices in a mesh: slab: 4 (over y_hi, core), wide: 128 (over y_lo, z, x).
Axes of the slice: x: 4, y: 4 (y_hi: 2, y_lo: 2; y = y_hi * 2 + y_lo), z: 16, core: 2. Of those that a mesh axis runs over, the one named last changes fastest.
Arguments:
- spectrum: float32 [1152, 512, 128], P('wide', 'slab'), may hold values from 0 to 1
- sea_mask: int32 [512, 128], P('slab'), may hold values 0 or 1
- courant: float32 [32], replicated, may hold values from 0.05 to 0.7
- slot_owner: int32 [1152], replicated, may hold values from 0 to 1151, each once
- coupling: bfloat16 [1152, 1152], replicated, may hold values from -0.1875 to 0.1875
Outputs:
- evolved: float32 [1152, 512, 128], P('wide', 'slab')
Inputs may be any that keep to these rules, and one draw needn't show every extreme that they name: `slot_owner`: each component occurs in exactly one slot; component f * 36 + d has direction d and frequency f. `sea_mask`: 1 marks a sea point.
All inputs are finite; a program needn't handle non-finite values. No bound on the sum of `sea_mask` on one device may be relied on, other than what follows from the above.
Results may differ from a plain program's by a relative error of at most 0.0015.
Values sent between devices are 32-bit elements; how exact they have to be, the bound alone decides.
A program may use at most 64 MiB of HBM per device.

v0:
```python
import math

import jax
import jax.numpy as jnp
from jax import lax
from jax.sharding import PartitionSpec as P

ND = 36
STEPS = 2


time_step = 0.5


def split_up(value, dim, count):
    lengths = value.shape
    tiles = value.reshape(*lengths[:dim], count, lengths[dim] // count, *lengths[dim + 1 :])
    return jnp.moveaxis(tiles, dim, 0)


def edges_of(length, count):
    lap = length // count
    if lap >= 8:
        lap -= lap % 8
    return [lap * k for k in range(1, count)]


def laid_out(tiles, dim):
    tiles = jnp.moveaxis(tiles, 0, dim)
    lengths = tiles.shape
    return tiles.reshape(*lengths[:dim], lengths[dim] * lengths[dim + 1], *lengths[dim + 2 :])


def exchange_in_pieces(value, axis, pieces, split_dim, concat_dim):
    tiles = split_up(value, split_dim, lax.axis_size(axis))
    split_at = max(range(1, max(2, tiles.ndim - 1)), key=lambda d: tiles.shape[d])
    finished = []
    for section in jnp.split(tiles, edges_of(tiles.shape[split_at], pieces), axis=split_at):
        if section.size:
            finished.append(lax.all_to_all(section, axis, split_axis=0, concat_axis=0, tiled=True))
    return laid_out(jnp.concatenate(finished, axis=split_at), concat_dim)


def with_halo(value, sides, width):
    edges = {}
    for axis, dim in sides:
        count, length = (lax.axis_size(axis), value.shape[dim])
        up = [(i, (i + 1) % count) for i in range(count - 1)]
        last = lax.slice_in_dim(value, length - width, length, axis=dim)
        first = lax.slice_in_dim(value, 0, width, axis=dim)
        edges[dim] = (
            lax.ppermute(last, axis, up),
            lax.ppermute(first, axis, [(b, a) for a, b in up]),
        )
    done = []
    for _, dim in sides:
        low, high = edges[dim]
        around = [(width, width) if d in done else (0, 0) for d in range(value.ndim)]
        value = jnp.concatenate([jnp.pad(low, around), value, jnp.pad(high, around)], axis=dim)
        done.append(dim)
    return value


def velocities(slot_owner, courant):
    band_count = courant.shape[0]
    heading = slot_owner % ND
    freq_band = slot_owner // ND
    picked = freq_band[:, None] == jnp.arange(band_count, dtype=jnp.int32)[None, :]
    wave_speed = jnp.sum(jnp.where(picked, courant[None, :], 0.0), axis=1)
    wave_angle = heading.astype(jnp.float32) * (2.0 * math.pi / ND)
    return (wave_speed * jnp.cos(wave_angle), wave_speed * jnp.sin(wave_angle))


def combine_sides(energy, west_side, east_side, south_side, north_side, east_speed, north_speed):
    east_speed = east_speed[:, None, None]
    north_speed = north_speed[:, None, None]
    remain = 1.0 - jnp.abs(east_speed) - jnp.abs(north_speed)
    result = remain * energy + jnp.maximum(east_speed, 0.0) * west_side
    result = result + jnp.maximum(-east_speed, 0.0) * east_side
    result = result + jnp.maximum(north_speed, 0.0) * south_side
    return result + jnp.maximum(-north_speed, 0.0) * north_side


def advect(energy, padded, east_speed, north_speed):
    west_side = jnp.roll(energy, 1, axis=2)
    east_side = jnp.roll(energy, -1, axis=2)
    return combine_sides(
        energy, west_side, east_side, padded[:, :-2, :], padded[:, 2:, :], east_speed, north_speed
    )


def interact(moved, slot_table):
    slot_count = moved.shape[0]
    flattened = moved.reshape(slot_count, -1)
    rounded = flattened.astype(jnp.bfloat16)
    square = (flattened * flattened).astype(jnp.bfloat16)
    gain_term = flattened * jnp.dot(slot_table, rounded, preferred_element_type=jnp.float32)
    loss_term = lax.dot_general(
        slot_table, square, (((0,), (0,)), ((), ())), preferred_element_type=jnp.float32
    )
    updated = jnp.maximum(flattened + time_step * (gain_term - loss_term), 0.0)
    return updated.reshape(moved.shape)


def body(spectrum, sea_mask, courant, slot_owner, coupling):
    wide_index = lax.axis_index("wide")
    wide_count = lax.axis_size("wide")
    sea_float = sea_mask.astype(jnp.float32)
    slot_table = jnp.take(jnp.take(coupling, slot_owner, axis=0), slot_owner, axis=1)
    energy = spectrum * sea_float[None]
    row_count = energy.shape[1] // wide_count
    local_sea = lax.dynamic_slice_in_dim(sea_float, wide_index * row_count, row_count, 0)
    east_speed, north_speed = velocities(slot_owner, courant)
    energy = exchange_in_pieces(energy, "wide", 2, 1, 0)
    for repeat in range(STEPS):
        padded = with_halo(energy, ((("slab", "wide"), 1),), 1)
        moved = advect(energy, padded, east_speed, north_speed)
        energy = interact(moved, slot_table) * local_sea[None]
    return lax.all_to_all(energy, "wide", split_axis=0, concat_axis=1, tiled=True)


def solution(mesh):
    return jax.shard_map(
        body,
        mesh=mesh,
        in_specs=(P("wide", "slab", None), P("slab", None), P(), P(), P()),
        out_specs=P("wide", "slab", None),
        check_vma=False,
    )
```

profile of v0, /device:TPU:1, one launch (start us, length us, event | category | flops | bytes accessed | tf_op | source)
XLA Modules:
  0.0 181.7 jit_solution(6256171248074179696)
XLA Ops:
  0.0 1.0 convert_element_type.19
  1.0 1.4 fusion.11
  2.5 1.0 copy-done.1
  3.4 0.8 split.8
  4.2 21.3 %all-to-all-start = ((f32[128,4,1,128]{3,1,2,0:T(4,128)}), f32[128,4,1,128]{3,1,2,0:T(4,128)S(1)}, u32[]{:S(2)}, u32[]{:S(2)}) async-start(f32[128,4,1,128]{3,1,2,0:T(4,128)} %split.8), calls=%async_computation | async-start | bytes 524288 | tf_op jit(solution)/shard_map/all_to_all | solution.py:40
  25.5 1.3 split.9
  26.8 1.1 copy.66
  27.9 5.1 %gather_fusion = bf16[1152,1152]{1,0:T(8,128)(2,1)} fusion(bf16[1152,1152]{1,0:T(8,128)(2,1)S(1)} %copy-done, s32[2048]{0:T(1024)S(1)} %pad_clamp_fusion), kind=kCustom, calls=%fused_computation | custom fusion | bytes 5313024 | tf_op jit(solution)/shard_map/jit(_take)/gather | solution.py:109
  33.0 14.0 %all-to-all-done = f32[128,4,1,128]{3,1,2,0:T(4,128)S(1)} async-done(((f32[128,4,1,128]{3,1,2,0:T(4,128)}), f32[128,4,1,128]{3,1,2,0:T(4,128)S(1)}, u32[]{:S(2)}, u32[]{:S(2)}) %all-to-all-start) | async-done | bytes 262176 | tf_op jit(solution)/shard_map/all_to_all | solution.py:40
  47.0 7.2 %all-to-all-start.1 = ((f32[128,5,1,128]{3,2,1,0:T(1,128)}), f32[128,5,1,128]{3,2,1,0:T(1,128)S(1)}, u32[]{:S(2)}, u32[]{:S(2)}) async-start(f32[128,5,1,128]{3,2,1,0:T(1,128)} %copy.66), calls=%async_computation.1 | async-start | bytes 655360 | tf_op jit(solution)/shard_map/all_to_all | solution.py:40
  54.2 3.7 %broadcast_select_fusion = bf16[1152,1152]{1,0:T(8,128)(2,1)} fusion(bf16[1152,1152]{1,0:T(8,128)(2,1)} %gather_fusion, pred[1152]{0:T(1024)(128)(4,1)S(1)} %compare_and_fusion), kind=kLoop, calls=%fused_computation.2 | loop fusion | flops 1327104 | bytes 5309568 | tf_op jit(solution)/shard_map/jit(_take)/select_n | solution.py:109
  57.9 5.2 %copy.75 = bf16[1152,1152]{0,1:T(8,128)(2,1)} copy(bf16[1152,1152]{1,0:T(8,128)(2,1)} %broadcast_select_fusion) | data formatting | bytes 5308416 | tf_op jit(solution)/shard_map/jit(_take)/select_n | solution.py:109
  63.1 9.2 %gather_fusion.1 = bf16[1152,1152]{1,0:T(8,128)(2,1)} fusion(bf16[1152,1152]{0,1:T(8,128)(2,1)} %copy.75, s32[2048]{0:T(1024)S(1)} %pad_clamp_fusion), kind=kCustom, calls=%fused_computation.1 | custom fusion | bytes 5313024 | tf_op jit(solution)/shard_map/jit(_take)/gather | solution.py:109
  72.6 4.3 %all-to-all-done.1 = f32[128,5,1,128]{3,2,1,0:T(1,128)S(1)} async-done(((f32[128,5,1,128]{3,2,1,0:T(1,128)}), f32[128,5,1,128]{3,2,1,0:T(1,128)S(1)}, u32[]{:S(2)}, u32[]{:S(2)}) %all-to-all-start.1) | async-done | bytes 327712 | tf_op jit(solution)/shard_map/all_to_all | solution.py:40
  76.9 1.3 pad_maximum_fusion
  78.2 1.4 copy.68
  79.6 7.4 %collective-permute-start.1 = (f32[1152,1,128]{0,2,1:T(8,128)S(1)}, f32[1152,1,128]{0,2,1:T(8,128)S(1)}, u32[]{:S(2)}, u32[]{:S(2)}) collective-permute-start(f32[1152,1,128]{0,2,1:T(8,128)S(1)} %copy.68), channel_id=1, source_target_pairs={{1,0},{2,1},{3,2},{4,3},{5,4},{6,5},{7,6},{8,7},{9,8},{10,9},{11,1... | collective-permute-start | bytes 1769480 | tf_op jit(solution)/shard_map/ppermute | solution.py:53
  87.1 1.9 %collective-permute-start = (f32[1152,1,128]{0,2,1:T(8,128)S(1)}, f32[1152,1,128]{0,2,1:T(8,128)S(1)}, u32[]{:S(2)}, u32[]{:S(2)}) collective-permute-start(f32[1152,1,128]{0,2,1:T(8,128)S(1)} %copy.68), channel_id=1, source_target_pairs={{0,1},{1,2},{2,3},{3,4},{4,5},{5,6},{6,7},{7,8},{8,9},{9,10},{10,1... | collective-permute-start | bytes 1769480 | tf_op jit(solution)/shard_map/ppermute | solution.py:52
  89.1 4.8 %collective-permute-done.1 = f32[1152,1,128]{0,2,1:T(8,128)S(1)} collective-permute-done((f32[1152,1,128]{0,2,1:T(8,128)S(1)}, f32[1152,1,128]{0,2,1:T(8,128)S(1)}, u32[]{:S(2)}, u32[]{:S(2)}) %collective-permute-start.1) | collective-permute-done | bytes 589856 | tf_op jit(solution)/shard_map/ppermute | solution.py:53
  93.9 14.7 %collective-permute-done = f32[1152,1,128]{0,2,1:T(8,128)S(1)} collective-permute-done((f32[1152,1,128]{0,2,1:T(8,128)S(1)}, f32[1152,1,128]{0,2,1:T(8,128)S(1)}, u32[]{:S(2)}, u32[]{:S(2)}) %collective-permute-start) | collective-permute-done | bytes 589856 | tf_op jit(solution)/shard_map/ppermute | solution.py:52
  108.5 0.3 fusion.16
  108.8 1.0 fusion.23
  109.8 0.9 fusion.9
  110.7 1.9 %collective-permute-start.3 = (f32[1152,1,128]{0,2,1:T(8,128)S(1)}, f32[1152,1,128]{0,2,1:T(8,128)S(1)}, u32[]{:S(2)}, u32[]{:S(2)}) collective-permute-start(f32[1152,1,128]{0,2,1:T(8,128)S(1)} %bitcast.37), channel_id=1, source_target_pairs={{1,0},{2,1},{3,2},{4,3},{5,4},{6,5},{7,6},{8,7},{9,8},{10,9},{11,1... | collective-permute-start | bytes 1769480 | tf_op jit(solution)/shard_map/ppermute | solution.py:53
  112.6 3.5 %collective-permute-start.2 = (f32[1152,1,128]{0,2,1:T(8,128)S(1)}, f32[1152,1,128]{0,2,1:T(8,128)S(1)}, u32[]{:S(2)}, u32[]{:S(2)}) collective-permute-start(f32[1152,1,128]{0,2,1:T(8,128)S(1)} %bitcast.38), channel_id=1, source_target_pairs={{0,1},{1,2},{2,3},{3,4},{4,5},{5,6},{6,7},{7,8},{8,9},{9,10},{10,1... | collective-permute-start | bytes 1769480 | tf_op jit(solution)/shard_map/ppermute | solution.py:52
  116.3 6.3 %collective-permute-done.3 = f32[1152,1,128]{0,2,1:T(8,128)S(1)} collective-permute-done((f32[1152,1,128]{0,2,1:T(8,128)S(1)}, f32[1152,1,128]{0,2,1:T(8,128)S(1)}, u32[]{:S(2)}, u32[]{:S(2)}) %collective-permute-start.3) | collective-permute-done | bytes 589856 | tf_op jit(solution)/shard_map/ppermute | solution.py:53
  122.6 11.5 %collective-permute-done.2 = f32[1152,1,128]{0,2,1:T(8,128)S(1)} collective-permute-done((f32[1152,1,128]{0,2,1:T(8,128)S(1)}, f32[1152,1,128]{0,2,1:T(8,128)S(1)}, u32[]{:S(2)}, u32[]{:S(2)}) %collective-permute-start.2) | collective-permute-done | bytes 589856 | tf_op jit(solution)/shard_map/ppermute | solution.py:52
  134.3 1.0 fusion.24
  135.4 1.7 fusion.10
  137.1 1.5 copy.78
  138.6 42.3 %all_to_all.28 = f32[1152,1,128]{2,1,0:T(1,128)S(1)} all-to-all(f32[1152,1,128]{2,1,0:T(1,128)S(1)} %copy.78), channel_id=1, replica_groups=mesh['slab'=4,'wide'=128] {'wide'}, dimensions={0} | all-to-all | bytes 1179648 | tf_op jit(solution)/shard_map/all_to_all | solution.py:119
  180.8 0.9 copy.86
  (20 shorter events, 0.6 us)
Async XLA Ops:
  0.0 27.9 %copy-start = (bf16[1152,1152]{1,0:T(8,128)(2,1)S(1)}, bf16[1152,1152]{1,0:T(8,128)(2,1)}, u32[]{:S(2)}) copy-start(bf16[1152,1152]{1,0:T(8,128)(2,1)} %param.9) | copy-start | bytes 7962628
  0.0 27.9 %copy-start.3 = (s32[1152]{0:T(1024)S(1)}, s32[1152]{0:T(1024)}, u32[]{:S(2)}) copy-start(s32[1152]{0:T(1024)} %param.8) | copy-start | bytes 13828
  2.5 1.0 copy-start.1
  4.2 42.8 %all-to-all-start = ((f32[128,4,1,128]{3,1,2,0:T(4,128)}), f32[128,4,1,128]{3,1,2,0:T(4,128)S(1)}, u32[]{:S(2)}, u32[]{:S(2)}) async-start(f32[128,4,1,128]{3,1,2,0:T(4,128)} %split.8), calls=%async_computation | async-start | bytes 524288 | tf_op jit(solution)/shard_map/all_to_all | solution.py:40
  47.0 29.9 %all-to-all-start.1 = ((f32[128,5,1,128]{3,2,1,0:T(1,128)}), f32[128,5,1,128]{3,2,1,0:T(1,128)S(1)}, u32[]{:S(2)}, u32[]{:S(2)}) async-start(f32[128,5,1,128]{3,2,1,0:T(1,128)} %copy.66), calls=%async_computation.1 | async-start | bytes 655360 | tf_op jit(solution)/shard_map/all_to_all | solution.py:40
  63.1 9.3 %copy-start.4 = (f32[32]{0:T(128)S(1)}, f32[32]{0:T(128)}, u32[]{:S(2)}) copy-start(f32[32]{0:T(128)} %param.7) | copy-start | bytes 388
  79.6 14.2 %collective-permute-start.1 = (f32[1152,1,128]{0,2,1:T(8,128)S(1)}, f32[1152,1,128]{0,2,1:T(8,128)S(1)}, u32[]{:S(2)}, u32[]{:S(2)}) collective-permute-start(f32[1152,1,128]{0,2,1:T(8,128)S(1)} %copy.68), channel_id=1, source_target_pairs={{1,0},{2,1},{3,2},{4,3},{5,4},{6,5},{7,6},{8,7},{9,8},{10,9},{11,1... | collective-permute-start | bytes 1769480 | tf_op jit(solution)/shard_map/ppermute | solution.py:53
  87.1 21.5 %collective-permute-start = (f32[1152,1,128]{0,2,1:T(8,128)S(1)}, f32[1152,1,128]{0,2,1:T(8,128)S(1)}, u32[]{:S(2)}, u32[]{:S(2)}) collective-permute-start(f32[1152,1,128]{0,2,1:T(8,128)S(1)} %copy.68), channel_id=1, source_target_pairs={{0,1},{1,2},{2,3},{3,4},{4,5},{5,6},{6,7},{7,8},{8,9},{9,10},{10,1... | collective-permute-start | bytes 1769480 | tf_op jit(solution)/shard_map/ppermute | solution.py:52
  89.0 19.8 %copy-start.2 = (bf16[1152,1152]{1,0:T(8,128)(2,1)S(1)}, bf16[1152,1152]{1,0:T(8,128)(2,1)}, u32[]{:S(2)}) copy-start(bf16[1152,1152]{1,0:T(8,128)(2,1)} %gather_fusion.1) | copy-start | bytes 7962628
  110.7 11.9 %collective-permute-start.3 = (f32[1152,1,128]{0,2,1:T(8,128)S(1)}, f32[1152,1,128]{0,2,1:T(8,128)S(1)}, u32[]{:S(2)}, u32[]{:S(2)}) collective-permute-start(f32[1152,1,128]{0,2,1:T(8,128)S(1)} %bitcast.37), channel_id=1, source_target_pairs={{1,0},{2,1},{3,2},{4,3},{5,4},{6,5},{7,6},{8,7},{9,8},{10,9},{11,1... | collective-permute-start | bytes 1769480 | tf_op jit(solution)/shard_map/ppermute | solution.py:53
  112.6 21.5 %collective-permute-start.2 = (f32[1152,1,128]{0,2,1:T(8,128)S(1)}, f32[1152,1,128]{0,2,1:T(8,128)S(1)}, u32[]{:S(2)}, u32[]{:S(2)}) collective-permute-start(f32[1152,1,128]{0,2,1:T(8,128)S(1)} %bitcast.38), channel_id=1, source_target_pairs={{0,1},{1,2},{2,3},{3,4},{4,5},{5,6},{6,7},{7,8},{8,9},{9,10},{10,1... | collective-permute-start | bytes 1769480 | tf_op jit(solution)/shard_map/ppermute | solution.py:52
where the time goes:
time: 182 us
  waiting for transfers between devices  55.5 us (30%)
  starting transfers between devices  43.4 us (24%)
  blocking collectives  42.3 us (23%)
  local copies, waits for them, and re-layouts  27.6 us (15%)
  other arithmetic  8.13 us (4%)
  matrix products  4.62 us (3%)
    all_to_all x1, blocking collectives, body(): lax.all_to_all(energy, 'wide', split_axis=0, concat_axis=1, tiled=True)  42.3 us
    all_to_all x2, starting transfers between devices, exchange_in_pieces(): lax.all_to_all(section, axis, split_axis=0, concat_axis=0, tiled=True)  28.6 us
    ppermute x2, waiting for transfers between devices, with_halo(): lax.ppermute(last, axis, up)  26.2 us
    all_to_all x2, waiting for transfers between devices, exchange_in_pieces(): lax.all_to_all(section, axis, split_axis=0, concat_axis=0, tiled=True)  18.3 us
    ppermute x2, waiting for transfers between devices, with_halo(): lax.ppermute(first, axis, [(b, a) for a, b in up])  11 us
    ppermute x2, starting transfers between devices, with_halo(): lax.ppermute(first, axis, [(b, a) for a, b in up])  9.34 us
    gather x1, local copies, waits for them, and re-layouts, body(): jnp.take(jnp.take(coupling, slot_owner, axis=0), slot_owner, axis=1)  9.24 us
    ppermute x2, starting transfers between devices, with_halo(): lax.ppermute(last, axis, up)  5.46 us
  transfers between devices with their start and end apart: 6, of which 6 were waited for; matrix products, arithmetic and copies ran while one was open for 14% of the time, Pallas kernels for 0%

commit v1 on v0

--- a/solution.py
+++ b/solution.py
@@ -3,6 +3,8 @@
 import jax
 import jax.numpy as jnp
 from jax import lax
+from jax.experimental import pallas as pl
+from jax.experimental.pallas import tpu as pltpu
 from jax.sharding import PartitionSpec as P
 
 ND = 36
@@ -12,33 +14,74 @@
 time_step = 0.5
 
 
-def split_up(value, dim, count):
-    lengths = value.shape
-    tiles = value.reshape(*lengths[:dim], count, lengths[dim] // count, *lengths[dim + 1 :])
-    return jnp.moveaxis(tiles, dim, 0)
+WIDE = 128
+OWN = 9
+PAD = 16
 
 
-def edges_of(length, count):
-    lap = length // count
-    if lap >= 8:
-        lap -= lap % 8
-    return [lap * k for k in range(1, count)]
+def peer_of(me, step):
+    y, z, x = me // 64, (me // 4) % 16, me % 4
+    turn, plane = step % 16, step // 16
+    half = (turn + 1) // 2
+    dz = jnp.where(turn % 2 == 1, half, 16 - half)
+    return ((y + plane // 4) % 2) * 64 + ((z + dz) % 16) * 4 + (x + plane % 4) % 4
 
 
-def laid_out(tiles, dim):
-    tiles = jnp.moveaxis(tiles, 0, dim)
-    lengths = tiles.shape
-    return tiles.reshape(*lengths[:dim], lengths[dim] * lengths[dim + 1], *lengths[dim + 2 :])
+def transpose_kernel(x_ref, o_ref, outbox, inbox, send_sem, recv_sem):
+    me = lax.axis_index("wide")
+    barrier = pltpu.get_barrier_semaphore()
+
+    def greet(step, carry):
+        pl.semaphore_signal(
+            barrier, inc=1, device_id={"wide": peer_of(me, step)}, device_id_type=pl.DeviceIdType.MESH
+        )
+        return carry
+
+    lax.fori_loop(1, WIDE, greet, 0)
+    for j in range(OWN):
+        outbox[pl.ds(j, WIDE, stride=PAD), :] = x_ref[j]
+    pl.semaphore_wait(barrier, WIDE - 1)
+    mine = pl.ds(pl.multiple_of(me * PAD, PAD), OWN)
+
+    def send(step, carry):
+        peer = peer_of(me, step)
+        pltpu.make_async_remote_copy(
+            src_ref=outbox.at[pl.ds(pl.multiple_of(peer * PAD, PAD), OWN)],
+            dst_ref=inbox.at[mine],
+            send_sem=send_sem,
+            recv_sem=recv_sem,
+            device_id={"wide": peer},
+            device_id_type=pl.DeviceIdType.MESH,
+        ).start()
+        return carry
+
+    lax.fori_loop(1, WIDE, send, 0)
+    pltpu.make_async_copy(outbox.at[mine], inbox.at[mine], recv_sem).start()
+    pltpu.make_async_copy(x_ref, x_ref, recv_sem).wait()
+    for j in range(OWN):
+        o_ref[j] = inbox[pl.ds(j, WIDE, stride=PAD), :]
+    most = x_ref.at[pl.ds(0, OWN - 1)]
+    pltpu.make_async_copy(most, most, send_sem).wait()
+    rest = x_ref.at[0, pl.ds(0, WIDE - OWN)]
+    pltpu.make_async_copy(rest, rest, send_sem).wait()
 
 
-def exchange_in_pieces(value, axis, pieces, split_dim, concat_dim):
-    tiles = split_up(value, split_dim, lax.axis_size(axis))
-    split_at = max(range(1, max(2, tiles.ndim - 1)), key=lambda d: tiles.shape[d])
-    finished = []
-    for section in jnp.split(tiles, edges_of(tiles.shape[split_at], pieces), axis=split_at):
-        if section.size:
-            finished.append(lax.all_to_all(section, axis, split_axis=0, concat_axis=0, tiled=True))
-    return laid_out(jnp.concatenate(finished, axis=split_at), concat_dim)
+def transpose_over_wide(value, collective_id):
+    return pl.pallas_call(
+        transpose_kernel,
+        out_shape=jax.ShapeDtypeStruct((OWN, WIDE, 128), jnp.float32),
+        in_specs=[pl.BlockSpec(memory_space=pltpu.VMEM)],
+        out_specs=pl.BlockSpec(memory_space=pltpu.VMEM),
+        scratch_shapes=[
+            pltpu.VMEM((WIDE * PAD, 128), jnp.float32),
+            pltpu.VMEM((WIDE * PAD, 128), jnp.float32),
+            pltpu.SemaphoreType.DMA,
+            pltpu.SemaphoreType.DMA,
+        ],
+        compiler_params=pltpu.CompilerParams(
+            collective_id=collective_id, has_side_effects=True, vmem_limit_bytes=16 << 20
+        ),
+    )(value)
 
 
 def with_halo(value, sides, width):
@@ -104,19 +147,17 @@
 
 def body(spectrum, sea_mask, courant, slot_owner, coupling):
     wide_index = lax.axis_index("wide")
-    wide_count = lax.axis_size("wide")
     sea_float = sea_mask.astype(jnp.float32)
+    slot_owner = slot_owner.reshape(WIDE, OWN).T.reshape(-1)
     slot_table = jnp.take(jnp.take(coupling, slot_owner, axis=0), slot_owner, axis=1)
-    energy = spectrum * sea_float[None]
-    row_count = energy.shape[1] // wide_count
-    local_sea = lax.dynamic_slice_in_dim(sea_float, wide_index * row_count, row_count, 0)
+    local_sea = lax.dynamic_slice_in_dim(sea_float, wide_index, 1, 0)
     east_speed, north_speed = velocities(slot_owner, courant)
-    energy = exchange_in_pieces(energy, "wide", 2, 1, 0)
+    energy = transpose_over_wide(spectrum * sea_float[None], 0).reshape(OWN * WIDE, 1, 128)
     for repeat in range(STEPS):
         padded = with_halo(energy, ((("slab", "wide"), 1),), 1)
         moved = advect(energy, padded, east_speed, north_speed)
         energy = interact(moved, slot_table) * local_sea[None]
-    return lax.all_to_all(energy, "wide", split_axis=0, concat_axis=1, tiled=True)
+    return transpose_over_wide(energy.reshape(OWN, WIDE, 128), 1)
 
 
 def solution(mesh):

time: 182 us -> 170 us (0.934)
  Pallas kernels: 0 us -> 93.4 us
  blocking collectives: 42.3 us -> 0 us
  waiting for transfers between devices: 55.5 us -> 17.9 us
  starting transfers between devices: 43.4 us -> 20.8 us
  local copies, waits for them, and re-layouts: 27.6 us -> 24.4 us
    pallas_call x0 -> x2, Pallas kernels: none -> 93.4 us  [transpose_over_wide(): pl.pallas_call(transpose_kernel, out_shape=jax.ShapeDtypeStruct((OWN, WID...]
    all_to_all x1 -> x0, blocking collectives: 42.3 us -> none  [body(): lax.all_to_all(energy, 'wide', split_axis=0, concat_axis=1, tiled=True)]
    all_to_all x2 -> x0, starting transfers between devices: 28.6 us -> none  [exchange_in_pieces(): lax.all_to_all(section, axis, split_axis=0, concat_axis=0, tiled=True)]
    all_to_all x2 -> x0, waiting for transfers between devices: 18.3 us -> none  [exchange_in_pieces(): lax.all_to_all(section, axis, split_axis=0, concat_axis=0, tiled=True)]
    ppermute x2, waiting for transfers between devices: 26.2 us -> 12.8 us  [with_halo(): lax.ppermute(last, axis, up)]
    ppermute x2, starting transfers between devices: 9.34 us -> 16.9 us  [with_halo(): lax.ppermute(first, axis, [(b, a) for a, b in up])]
    ppermute x2, waiting for transfers between devices: 11 us -> 5.1 us  [with_halo(): lax.ppermute(first, axis, [(b, a) for a, b in up])]
    split x3 -> x0, local copies, waits for them, and re-layouts: 3.1 us -> none  [exchange_in_pieces(): jnp.split(tiles, edges_of(tiles.shape[split_at], pieces), axis=split_at)]
  transfers between devices with their start and end apart: 6 -> 4, of which waited for: 6 -> 2; matrix products, arithmetic and copies ran while one was open for 14% -> 15% of each run, Pallas kernels for 0% -> 0%
where the time goes in v1:
time: 170 us; the launch traced here: 169 us
  Pallas kernels  93.4 us (55%)
  local copies, waits for them, and re-layouts  24.4 us (14%)
  starting transfers between devices  20.8 us (12%)
  waiting for transfers between devices  17.9 us (11%)
  other arithmetic  7.9 us (5%)
  matrix products  4.61 us (3%)
    pallas_call x2, Pallas kernels, transpose_over_wide(): pl.pallas_call(transpose_kernel, out_shape=jax.ShapeDtypeStruct((OWN, WID...  93.4 us
    ppermute x2, starting transfers between devices, with_halo(): lax.ppermute(first, axis, [(b, a) for a, b in up])  16.9 us
    ppermute x2, waiting for transfers between devices, with_halo(): lax.ppermute(last, axis, up)  12.8 us
    gather x1, local copies, waits for them, and re-layouts, body(): jnp.take(jnp.take(coupling, slot_owner, axis=0), slot_owner, axis=1)  9.3 us
    select_n x1, local copies, waits for them, and re-layouts, body(): jnp.take(coupling, slot_owner, axis=0)  5.21 us
    gather x1, local copies, waits for them, and re-layouts, body(): jnp.take(coupling, slot_owner, axis=0)  5.13 us
    ppermute x2, waiting for transfers between devices, with_halo(): lax.ppermute(first, axis, [(b, a) for a, b in up])  5.1 us
    ppermute x2, starting transfers between devices, with_halo(): lax.ppermute(last, axis, up)  3.84 us
  transfers between devices with their start and end apart: 4, of which 2 were waited for; matrix products, arithmetic and copies ran while one was open for 15% of the time, Pallas kernels for 0%

profile of v1, /device:TPU:1, one launch (start us, length us, event | category | flops | bytes accessed | tf_op | source)
XLA Modules:
  0.0 169.1 jit_solution(10382808931648122991)
XLA Ops:
  0.0 1.0 convert_element_type.35
  1.0 1.1 broadcast_multiply_fusion.x_ref
  2.1 52.9 %shard_map.55 = f32[9,128,128]{2,1,0:T(8,128)S(1)} custom-call(f32[9,128,128]{2,1,0:T(8,128)S(1)} %broadcast_multiply_fusion.x_ref), custom_call_target="tpu_custom_call" | custom-call | tf_op jit(solution)/shard_map/pallas_call | solution.py:70
  55.0 1.1 copy.31
  56.1 9.1 %collective-permute-start.1 = (f32[1152,1,128]{0,2,1:T(8,128)}, f32[1152,1,128]{0,2,1:T(8,128)}, u32[]{:S(2)}, u32[]{:S(2)}) collective-permute-start(f32[1152,1,128]{0,2,1:T(8,128)} %copy.31), channel_id=1, source_target_pairs={{1,0},{2,1},{3,2},{4,3},{5,4},{6,5},{7,6},{8,7},{9,8},{10,9},{11,1... | collective-permute-start | bytes 1769480 | tf_op jit(solution)/shard_map/ppermute | solution.py:96
  65.2 1.9 %collective-permute-start = (f32[1152,1,128]{0,2,1:T(8,128)}, f32[1152,1,128]{0,2,1:T(8,128)}, u32[]{:S(2)}, u32[]{:S(2)}) collective-permute-start(f32[1152,1,128]{0,2,1:T(8,128)} %copy.31), channel_id=1, source_target_pairs={{0,1},{1,2},{2,3},{3,4},{4,5},{5,6},{6,7},{7,8},{8,9},{9,10},{10,1... | collective-permute-start | bytes 1769480 | tf_op jit(solution)/shard_map/ppermute | solution.py:95
  67.1 0.2 reshape.292
  67.3 0.1 copy.30
  67.4 0.8 fusion.32
  68.3 0.1 select_reduce_fusion
  68.4 0.1 abs_subtract_fusion
  68.4 5.1 %gather_fusion = bf16[1152,1152]{1,0:T(8,128)(2,1)} fusion(bf16[1152,1152]{1,0:T(8,128)(2,1)S(1)} %copy-done, s32[2048]{0:T(1024)S(1)} %pad_clamp_fusion), kind=kCustom, calls=%fused_computation | custom fusion | bytes 5313024 | tf_op jit(solution)/shard_map/jit(_take)/gather | solution.py:152
  73.6 3.7 %broadcast_select_fusion = bf16[1152,1152]{1,0:T(8,128)(2,1)} fusion(bf16[1152,1152]{1,0:T(8,128)(2,1)} %gather_fusion, pred[1152]{0:T(1024)(128)(4,1)S(1)} %compare_and_fusion), kind=kLoop, calls=%fused_computation.2 | loop fusion | flops 1327104 | bytes 5309568 | tf_op jit(solution)/shard_map/jit(_take)/select_n | solution.py:152
  77.2 5.2 %copy.39 = bf16[1152,1152]{0,1:T(8,128)(2,1)} copy(bf16[1152,1152]{1,0:T(8,128)(2,1)} %broadcast_select_fusion) | data formatting | bytes 5308416 | tf_op jit(solution)/shard_map/jit(_take)/select_n | solution.py:152
  82.4 9.3 %gather_fusion.1 = bf16[1152,1152]{1,0:T(8,128)(2,1)} fusion(bf16[1152,1152]{0,1:T(8,128)(2,1)} %copy.39, s32[2048]{0:T(1024)S(1)} %pad_clamp_fusion), kind=kCustom, calls=%fused_computation.1 | custom fusion | bytes 5313024 | tf_op jit(solution)/shard_map/jit(_take)/gather | solution.py:152
  91.8 0.1 fusion.31
  91.9 0.0 collective-permute-done
  91.9 1.7 fusion.14
  93.5 0.3 copy-done.2
  93.9 1.0 fusion.21
  94.9 0.9 fusion.9
  95.8 7.9 %collective-permute-start.3 = (f32[1152,1,128]{0,2,1:T(8,128)S(1)}, f32[1152,1,128]{0,2,1:T(8,128)S(1)}, u32[]{:S(2)}, u32[]{:S(2)}) collective-permute-start(f32[1152,1,128]{0,2,1:T(8,128)S(1)} %bitcast.72), channel_id=1, source_target_pairs={{1,0},{2,1},{3,2},{4,3},{5,4},{6,5},{7,6},{8,7},{9,8},{10,9},{11,1... | collective-permute-start | bytes 1769480 | tf_op jit(solution)/shard_map/ppermute | solution.py:96
  103.6 1.9 %collective-permute-start.2 = (f32[1152,1,128]{0,2,1:T(8,128)S(1)}, f32[1152,1,128]{0,2,1:T(8,128)S(1)}, u32[]{:S(2)}, u32[]{:S(2)}) collective-permute-start(f32[1152,1,128]{0,2,1:T(8,128)S(1)} %bitcast.73), channel_id=1, source_target_pairs={{0,1},{1,2},{2,3},{3,4},{4,5},{5,6},{6,7},{7,8},{8,9},{9,10},{10,1... | collective-permute-start | bytes 1769480 | tf_op jit(solution)/shard_map/ppermute | solution.py:95
  105.6 0.1 slice_bitcast_fusion
  105.7 5.1 %collective-permute-done.3 = f32[1152,1,128]{0,2,1:T(8,128)S(1)} collective-permute-done((f32[1152,1,128]{0,2,1:T(8,128)S(1)}, f32[1152,1,128]{0,2,1:T(8,128)S(1)}, u32[]{:S(2)}, u32[]{:S(2)}) %collective-permute-start.3) | collective-permute-done | bytes 589856 | tf_op jit(solution)/shard_map/ppermute | solution.py:96
  110.8 12.8 %collective-permute-done.2 = f32[1152,1,128]{0,2,1:T(8,128)S(1)} collective-permute-done((f32[1152,1,128]{0,2,1:T(8,128)S(1)}, f32[1152,1,128]{0,2,1:T(8,128)S(1)}, u32[]{:S(2)}, u32[]{:S(2)}) %collective-permute-start.2) | collective-permute-done | bytes 589856 | tf_op jit(solution)/shard_map/ppermute | solution.py:95
  123.5 0.2 fusion.20
  123.8 1.0 fusion.22
  124.8 1.7 %fusion.4 = f32[1152,128]{0,1:T(8,128)} fusion(f32[1152,128]{0,1:T(8,128)S(1)} %fusion.20, f32[1152,128]{0,1:T(8,128)S(1)} %fusion.22, f32[128]{0:T(128)S(1)} %dynamic-slice_bitcast_fusion, bf16[1152,1152]{1,0:T(8,128)(2,1)S(1)} %copy-done.2, pred[1152]{0:T(1024)(128)(4,1)S(1)} %compare_and_fusion), kind=kOutput, calls=%fused_computation.9 | convolution fusion | flops 342097920 | bytes 4425344 | tf_op jit(solution)/shard_map/dot_general | solution.py:140
  126.5 1.3 copy.42
  127.8 40.5 %shard_map.56 = f32[9,128,128]{2,1,0:T(8,128)S(1)} custom-call(f32[9,128,128]{2,1,0:T(8,128)S(1)} %bitcast.71), custom_call_target="tpu_custom_call" | custom-call | tf_op jit(solution)/shard_map/pallas_call | solution.py:70
  168.3 0.8 copy.48
  (16 shorter events, 0.1 us)
Async XLA Ops:
  0.0 68.4 %copy-start = (bf16[1152,1152]{1,0:T(8,128)(2,1)S(1)}, bf16[1152,1152]{1,0:T(8,128)(2,1)}, u32[]{:S(2)}) copy-start(bf16[1152,1152]{1,0:T(8,128)(2,1)} %param.9) | copy-start | bytes 7962628
  0.0 67.1 %copy-start.3 = (s32[1152]{0:T(1024)S(1)}, s32[1152]{0:T(1024)}, u32[]{:S(2)}) copy-start(s32[1152]{0:T(1024)} %param.8) | copy-start | bytes 13828
  0.0 68.3 %copy-start.4 = (f32[32]{0:T(128)S(1)}, f32[32]{0:T(128)}, u32[]{:S(2)}) copy-start(f32[32]{0:T(128)} %param.7) | copy-start | bytes 388
  56.1 35.8 %collective-permute-start.1 = (f32[1152,1,128]{0,2,1:T(8,128)}, f32[1152,1,128]{0,2,1:T(8,128)}, u32[]{:S(2)}, u32[]{:S(2)}) collective-permute-start(f32[1152,1,128]{0,2,1:T(8,128)} %copy.31), channel_id=1, source_target_pairs={{1,0},{2,1},{3,2},{4,3},{5,4},{6,5},{7,6},{8,7},{9,8},{10,9},{11,1... | collective-permute-start | bytes 1769480 | tf_op jit(solution)/shard_map/ppermute | solution.py:96
  65.2 26.7 %collective-permute-start = (f32[1152,1,128]{0,2,1:T(8,128)}, f32[1152,1,128]{0,2,1:T(8,128)}, u32[]{:S(2)}, u32[]{:S(2)}) collective-permute-start(f32[1152,1,128]{0,2,1:T(8,128)} %copy.31), channel_id=1, source_target_pairs={{0,1},{1,2},{2,3},{3,4},{4,5},{5,6},{6,7},{7,8},{8,9},{9,10},{10,1... | collective-permute-start | bytes 1769480 | tf_op jit(solution)/shard_map/ppermute | solution.py:95
  82.4 9.3 %copy-start.1 = (f32[1152,1,128]{0,2,1:T(8,128)S(1)}, f32[1152,1,128]{0,2,1:T(8,128)}, u32[]{:S(2)}) copy-start(f32[1152,1,128]{0,2,1:T(8,128)} %copy.31) | copy-start | bytes 1769476
  91.8 2.1 %copy-start.2 = (bf16[1152,1152]{1,0:T(8,128)(2,1)S(1)}, bf16[1152,1152]{1,0:T(8,128)(2,1)}, u32[]{:S(2)}) copy-start(bf16[1152,1152]{1,0:T(8,128)(2,1)} %gather_fusion.1) | copy-start | bytes 7962628
  95.8 15.0 %collective-permute-start.3 = (f32[1152,1,128]{0,2,1:T(8,128)S(1)}, f32[1152,1,128]{0,2,1:T(8,128)S(1)}, u32[]{:S(2)}, u32[]{:S(2)}) collective-permute-start(f32[1152,1,128]{0,2,1:T(8,128)S(1)} %bitcast.72), channel_id=1, source_target_pairs={{1,0},{2,1},{3,2},{4,3},{5,4},{6,5},{7,6},{8,7},{9,8},{10,9},{11,1... | collective-permute-start | bytes 1769480 | tf_op jit(solution)/shard_map/ppermute | solution.py:96
  103.6 19.9 %collective-permute-start.2 = (f32[1152,1,128]{0,2,1:T(8,128)S(1)}, f32[1152,1,128]{0,2,1:T(8,128)S(1)}, u32[]{:S(2)}, u32[]{:S(2)}) collective-permute-start(f32[1152,1,128]{0,2,1:T(8,128)S(1)} %bitcast.73), channel_id=1, source_target_pairs={{0,1},{1,2},{2,3},{3,4},{4,5},{5,6},{6,7},{7,8},{8,9},{9,10},{10,1... | collective-permute-start | bytes 1769480 | tf_op jit(solution)/shard_map/ppermute | solution.py:95

commit v2 on v1

v2 whole, which is shorter than its diff:
```python
import math

import jax
import jax.numpy as jnp
from jax import lax
from jax.experimental import pallas as pl
from jax.experimental.pallas import tpu as pltpu
from jax.sharding import PartitionSpec as P

ND = 36
WIDE = 128
OWN = 9
PAD = 16
SLOTS = OWN * WIDE
ROWS = 128
HOLD = 144
TOP = 8
TILE = 16
GROUP = 144
HALF = 72
MESH = pl.DeviceIdType.MESH

time_step = 0.5


def place(me):
    return me // 64, (me // 4) % 16, me % 4


def tile_of(y, x):
    return jnp.where(y == 0, x, 7 - x)


def device_of(z, q):
    y = q // 4
    return y * 64 + z * 4 + jnp.where(y == 0, q, 7 - q)


def peer_of(me, step):
    y, z, x = place(me)
    turn, plane = step % 16, step // 16
    half = (turn + 1) // 2
    dz = jnp.where(turn % 2 == 1, half, 16 - half)
    return ((y + plane // 4) % 2) * 64 + ((z + dz) % 16) * 4 + (x + plane % 4) % 4


def swap_blocks(parts, block):
    parts = list(parts)
    for bit in (4, 2, 1):
        high = (block & bit) != 0
        for a in range(8):
            if a & bit:
                continue
            first, second = parts[a], parts[a + bit]
            parts[a] = jnp.where(high, pltpu.roll(second, TILE * bit, 1), first)
            parts[a + bit] = jnp.where(high, second, pltpu.roll(first, 128 - TILE * bit, 1))
    return parts


def kernel(
    spectrum,
    sea_mask,
    own_speed,
    slot_speed,
    owner,
    coupling,
    out,
    plane,
    table_in,
    outbox,
    inbox,
    outbox2,
    inbox2,
    rim_out,
    rim_in,
    picker,
    picker_t,
    half_table,
    table,
    table_t,
    owner_wide,
    east_wide,
    north_wide,
    moved,
    rounded,
    square,
    energy,
    row_out,
    row_in,
    col_out,
    col_in,
    load_sem,
    table_sem,
    send_sem,
    recv_sem,
    send_sem2,
    recv_sem2,
    rim_send,
    rim_recv,
    edge_send,
    edge_recv,
):
    slab = lax.axis_index("slab")
    me = lax.axis_index("wide")
    y, z, x = place(me)
    q = tile_of(y, x)
    spot = z * 8 + q
    up_slab, down_slab = (slab + 1) % 4, (slab + 3) % 4
    north_id = {
        "slab": jnp.where(z == 15, up_slab, slab),
        "wide": y * 64 + ((z + 1) % 16) * 4 + x,
    }
    south_id = {
        "slab": jnp.where(z == 0, down_slab, slab),
        "wide": y * 64 + ((z + 15) % 16) * 4 + x,
    }
    east_id = {"slab": slab, "wide": device_of(z, (q + 1) % 8)}
    west_id = {"slab": slab, "wide": device_of(z, (q + 7) % 8)}

    loads = pltpu.make_async_copy(spectrum, plane.at[:, pl.ds(TOP, ROWS)], load_sem)
    loads.start()
    table_load = pltpu.make_async_copy(coupling, table_in, table_sem)
    table_load.start()

    barrier = pltpu.get_barrier_semaphore()
    for there in (
        {"slab": up_slab, "wide": me},
        {"slab": down_slab, "wide": me},
        north_id,
        south_id,
    ):
        pl.semaphore_signal(barrier, inc=1, device_id=there, device_id_type=MESH)

    def greet(step, carry):
        pl.semaphore_signal(
            barrier, inc=1, device_id={"slab": slab, "wide": peer_of(me, step)}, device_id_type=MESH
        )
        return carry

    lax.fori_loop(1, WIDE, greet, 0)

    lane = lax.broadcasted_iota(jnp.int32, (8, 128), 1)
    block = lane // TILE

    loads.wait()
    sea = sea_mask[...].astype(jnp.float32)
    for j in range(OWN):
        plane[j, pl.ds(TOP, ROWS), :] = plane[j, pl.ds(TOP, ROWS), :] * sea
        plane[j, pl.ds(TOP - 8, 8), :] = jnp.zeros((8, 128), jnp.float32)
        plane[j, pl.ds(TOP + ROWS, 8), :] = jnp.zeros((8, 128), jnp.float32)
        rim_out[0, pl.ds(j, 1), :] = own_speed[3 * OWN + j] * plane[j, pl.ds(TOP + ROWS - 1, 1), :]
        rim_out[1, pl.ds(j, 1), :] = own_speed[4 * OWN + j] * plane[j, pl.ds(TOP, 1), :]

    def propagate(j, carry):
        remain = own_speed[j]
        east, west = own_speed[OWN + j], own_speed[2 * OWN + j]
        north, south = own_speed[3 * OWN + j], own_speed[4 * OWN + j]
        for h in range(2):
            parts = []
            for k in range(8):
                start = TOP + 8 * h + k
                here = plane[j, pl.ds(start, 8, stride=16), :]
                part = remain * here + east * pltpu.roll(here, 1, 1)
                part = part + west * pltpu.roll(here, 127, 1)
                part = part + north * plane[j, pl.ds(start - 1, 8, stride=16), :]
                parts.append(part + south * plane[j, pl.ds(start + 1, 8, stride=16), :])
            for k, part in enumerate(swap_blocks(parts, block)):
                outbox[pl.ds(h * 128 + k * PAD + j, 8, stride=256), :] = part
        return carry

    lax.fori_loop(0, OWN, propagate, 0)

    pl.semaphore_wait(barrier, WIDE - 1 + 4)

    rims = []
    for side, there in ((0, up_slab), (1, down_slab)):
        rims.append(
            pltpu.make_async_remote_copy(
                src_ref=rim_out.at[side, pl.ds(0, OWN)],
                dst_ref=rim_in.at[side, pl.ds(0, OWN)],
                send_sem=rim_send.at[side],
                recv_sem=rim_recv.at[side],
                device_id={"slab": there, "wide": me},
                device_id_type=MESH,
            )
        )
        rims[-1].start()
    for rim in rims:
        rim.wait()
    lane9 = lax.broadcasted_iota(jnp.int32, (OWN, 128), 1)
    below = jnp.where(slab > 0, 1.0, 0.0) * rim_in[0, pl.ds(0, OWN), :]
    above = jnp.where(slab < 3, 1.0, 0.0) * rim_in[1, pl.ds(0, OWN), :]
    for k in range(8):
        low = pltpu.roll(below, (128 - TILE * k) % 128, 1) if k else below
        rows = pl.ds(k * PAD, OWN)
        outbox[rows, :] = outbox[rows, :] + jnp.where(lane9 < TILE, low, 0.0)
        high = pltpu.roll(above, 112 - TILE * k, 1) if k < 7 else above
        rows = pl.ds((15 * 8 + k) * PAD, OWN)
        outbox[rows, :] = outbox[rows, :] + jnp.where(lane9 >= 112, high, 0.0)

    mine = pl.ds(pl.multiple_of(me * PAD, PAD), OWN)
    my_tile = pl.ds(pl.multiple_of(spot * PAD, PAD), OWN)

    def send(step, carry):
        peer = peer_of(me, step)
        py, pz, px = place(peer)
        row = (pz * 8 + tile_of(py, px)) * PAD
        pltpu.make_async_remote_copy(
            src_ref=outbox.at[pl.ds(pl.multiple_of(row, PAD), OWN)],
            dst_ref=inbox.at[mine],
            send_sem=send_sem,
            recv_sem=recv_sem,
            device_id={"slab": slab, "wide": peer},
            device_id_type=MESH,
        ).start()
        return carry

    lax.fori_loop(1, WIDE, send, 0)
    pltpu.make_async_copy(outbox.at[my_tile], inbox.at[mine], recv_sem).start()

    for j in range(OWN):
        rows = pl.ds(j * WIDE, WIDE)
        owner_wide[rows, :] = jnp.broadcast_to(owner[pl.ds(j, 1), :], (128, 128)).T
        east_wide[rows, :] = jnp.broadcast_to(slot_speed[pl.ds(j, 1), :], (128, 128)).T
        north_wide[rows, :] = jnp.broadcast_to(slot_speed[pl.ds(OWN + j, 1), :], (128, 128)).T

    lanes = lax.broadcasted_iota(jnp.int32, (128, 128), 1).astype(jnp.float32)
    sublanes = lax.broadcasted_iota(jnp.int32, (128, 128), 0).astype(jnp.float32)

    def pick(i, carry):
        rows = pl.ds(pl.multiple_of(i * 128, 128), 128)
        base = (i * 128).astype(jnp.float32)
        for j in range(OWN):
            columns = pl.ds(j * 128, 128)
            hit = owner_wide[rows, :] == lanes + 128.0 * j
            picker[rows, columns] = jnp.where(hit, 1.0, 0.0).astype(jnp.bfloat16)
            hit = owner[pl.ds(j, 1), :] == sublanes + base
            picker_t[rows, columns] = jnp.where(hit, 1.0, 0.0).astype(jnp.bfloat16)
        return carry

    lax.fori_loop(0, OWN, pick, 0)
    table_load.wait()

    def rows_picked(i, carry):
        rows = pl.ds(pl.multiple_of(i * 128, 128), 128)
        half_table[rows, :] = jnp.dot(
            picker[rows, :], table_in[...], preferred_element_type=jnp.float32
        ).astype(jnp.bfloat16)
        return carry

    lax.fori_loop(0, OWN, rows_picked, 0)

    def columns_picked(i, carry):
        rows = pl.ds(pl.multiple_of(i * 128, 128), 128)
        full = jnp.dot(half_table[rows, :], picker_t[...], preferred_element_type=jnp.float32)
        table[rows, :] = full.astype(jnp.bfloat16)
        for j in range(OWN):
            table_t[pl.ds(j * 128, 128), rows] = full[:, j * 128 : (j + 1) * 128].T.astype(jnp.bfloat16)
        return carry

    lax.fori_loop(0, OWN, columns_picked, 0)

    tile_sea = sea_mask[pl.ds(pl.multiple_of(z * 8, 8), 8), :].astype(jnp.float32)
    column = lax.broadcasted_iota(jnp.int32, (128, 128), 0)
    target = lax.broadcasted_iota(jnp.int32, (128, 128), 1)
    spread = jnp.where(column == q * TILE + target % TILE, 1.0, 0.0)
    tile_sea = jnp.dot(tile_sea, spread, preferred_element_type=jnp.float32)
    inner = lax.broadcasted_iota(jnp.int32, (8, 128), 0)
    tile_sea = jnp.sum(jnp.where(inner == block, tile_sea, 0.0), axis=0, keepdims=True)

    pltpu.make_async_copy(spectrum, spectrum, recv_sem).wait()
    for j in range(OWN):
        rows = pl.ds(j * WIDE, WIDE)
        value = inbox[pl.ds(j, WIDE, stride=PAD), :]
        moved[rows, :] = value
        rounded[rows, :] = value.astype(jnp.bfloat16)
        square[rows, :] = (value * value).astype(jnp.bfloat16)

    def interact(rows):
        value = moved[rows, :]
        gain = value * jnp.dot(table[rows, :], rounded[...], preferred_element_type=jnp.float32)
        loss = jnp.dot(table_t[rows, :], square[...], preferred_element_type=jnp.float32)
        return tile_sea * jnp.maximum(value + time_step * (gain - loss), 0.0)

    lane_g = lax.broadcasted_iota(jnp.int32, (GROUP, 128), 1)
    lane_h = lax.broadcasted_iota(jnp.int32, (HALF, 128), 1)
    for g in range(8):
        rows = pl.ds(g * GROUP, GROUP)
        value = interact(rows)
        energy[rows, :] = value
        north = pltpu.roll(value, (TILE * (g + 1)) % 128, 1) if g < 7 else value
        south = pltpu.roll(value, TILE * g, 1) if g else value
        here = lane_g // TILE == g
        if g:
            north = jnp.where(here, north, row_out[0])
            south = jnp.where(here, south, row_out[1])
        row_out[0] = north
        row_out[1] = south
        for u in range(2):
            b = 2 * g + u
            part = value[u * HALF : (u + 1) * HALF]
            east = pltpu.roll(part, (b + 113) % 128, 1) if b != 15 else part
            west = pltpu.roll(part, b, 1) if b else part
            here = lane_h % TILE == b
            if b:
                east = jnp.where(here, east, col_out[0])
                west = jnp.where(here, west, col_out[1])
            col_out[0] = east
            col_out[1] = west

    edges = []
    for e, (source, sink, side, there) in enumerate(
        (
            (row_out, row_in, 0, north_id),
            (row_out, row_in, 1, south_id),
            (col_out, col_in, 0, east_id),
            (col_out, col_in, 1, west_id),
        )
    ):
        edges.append(
            pltpu.make_async_remote_copy(
                src_ref=source.at[side],
                dst_ref=sink.at[side],
                send_sem=edge_send.at[e],
                recv_sem=edge_recv.at[e],
                device_id=there,
                device_id_type=MESH,
            )
        )
        edges[-1].start()
    for edge in edges:
        edge.wait()

    has_south = jnp.logical_or(slab > 0, z > 0)
    has_north = jnp.logical_or(slab < 3, z < 15)
    keep_south = jnp.where(has_south, 1.0, 0.0)
    keep_north = jnp.where(has_north, 1.0, 0.0)
    for b in range(16):
        g, u = b // 2, b % 2
        rows = pl.ds(b * HALF, HALF)
        packed = pl.ds(u * HALF, HALF)
        value = energy[rows, :]
        west = col_in[0]
        west = pltpu.roll(west, 128 - b, 1) if b else west
        west = jnp.where(lane_h % TILE == 0, west, pltpu.roll(value, 1, 1))
        east = col_in[1]
        east = pltpu.roll(east, 15 - b, 1) if b != 15 else east
        east = jnp.where(lane_h % TILE == TILE - 1, east, pltpu.roll(value, 127, 1))
        south = keep_south * row_in[0, packed, :]
        south = pltpu.roll(south, 128 - TILE * g, 1) if g else south
        south = jnp.where(lane_h < TILE, south, pltpu.roll(value, TILE, 1))
        north = keep_north * row_in[1, packed, :]
        north = pltpu.roll(north, 112 - TILE * g, 1) if g < 7 else north
        north = jnp.where(lane_h >= 112, north, pltpu.roll(value, 112, 1))
        e, n = east_wide[rows, :], north_wide[rows, :]
        result = (1.0 - jnp.abs(e) - jnp.abs(n)) * value + jnp.maximum(e, 0.0) * west
        result = result + jnp.maximum(-e, 0.0) * east
        result = result + jnp.maximum(n, 0.0) * south
        result = result + jnp.maximum(-n, 0.0) * north
        moved[rows, :] = result
    for j in range(OWN):
        rows = pl.ds(j * WIDE, WIDE)
        value = moved[rows, :]
        rounded[rows, :] = value.astype(jnp.bfloat16)
        square[rows, :] = (value * value).astype(jnp.bfloat16)
    for j in range(OWN):
        outbox2[pl.ds(j, WIDE, stride=PAD), :] = interact(pl.ds(j * WIDE, WIDE))

    def send_back(step, carry):
        peer = peer_of(me, step)
        pltpu.make_async_remote_copy(
            src_ref=outbox2.at[pl.ds(pl.multiple_of(peer * PAD, PAD), OWN)],
            dst_ref=inbox2.at[my_tile],
            send_sem=send_sem2,
            recv_sem=recv_sem2,
            device_id={"slab": slab, "wide": peer},
            device_id_type=MESH,
        ).start()
        return carry

    lax.fori_loop(1, WIDE, send_back, 0)
    pltpu.make_async_copy(outbox2.at[mine], inbox2.at[my_tile], recv_sem2).start()
    pltpu.make_async_copy(spectrum, spectrum, recv_sem2).wait()

    def unpack(j, carry):
        for h in range(2):
            parts = [inbox2[pl.ds(h * 128 + k * PAD + j, 8, stride=256), :] for k in range(8)]
            for k, part in enumerate(swap_blocks(parts, block)):
                out[j, pl.ds(8 * h + k, 8, stride=16), :] = part
        return carry

    lax.fori_loop(0, OWN, unpack, 0)
    for sem in (send_sem, send_sem2):
        most = plane.at[pl.ds(0, OWN - 1), pl.ds(0, ROWS)]
        pltpu.make_async_copy(most, most, sem).wait()
        rest = plane.at[0, pl.ds(0, ROWS - OWN)]
        pltpu.make_async_copy(rest, rest, sem).wait()


def velocities(slot_owner, courant):
    band_count = courant.shape[0]
    heading = slot_owner % ND
    freq_band = slot_owner // ND
    picked = freq_band[..., None] == jnp.arange(band_count, dtype=jnp.int32)
    wave_speed = jnp.sum(jnp.where(picked, courant, 0.0), axis=-1)
    wave_angle = heading.astype(jnp.float32) * (2.0 * math.pi / ND)
    return wave_speed * jnp.cos(wave_angle), wave_speed * jnp.sin(wave_angle)


def body(spectrum, sea_mask, courant, slot_owner, coupling):
    me = lax.axis_index("wide")
    east, north = velocities(lax.dynamic_slice_in_dim(slot_owner, me * OWN, OWN), courant)
    own_speed = jnp.concatenate(
        [
            1.0 - jnp.abs(east) - jnp.abs(north),
            jnp.maximum(east, 0.0),
            jnp.maximum(-east, 0.0),
            jnp.maximum(north, 0.0),
            jnp.maximum(-north, 0.0),
        ]
    )
    owner = slot_owner.reshape(WIDE, OWN).T
    slot_speed = jnp.concatenate(velocities(owner, courant))
    vmem = pl.BlockSpec(memory_space=pltpu.VMEM)
    anywhere = pl.BlockSpec(memory_space=pl.ANY)
    f32, bf16, dma = jnp.float32, jnp.bfloat16, pltpu.SemaphoreType.DMA
    mailbox = pltpu.VMEM((WIDE * PAD, 128), f32)
    square_table = pltpu.VMEM((SLOTS, SLOTS), bf16)
    column = pltpu.VMEM((SLOTS, 128), f32)
    return pl.pallas_call(
        kernel,
        out_shape=jax.ShapeDtypeStruct((OWN, ROWS, 128), f32),
        in_specs=[anywhere, vmem, pl.BlockSpec(memory_space=pltpu.SMEM), vmem, vmem, anywhere],
        out_specs=vmem,
        scratch_shapes=[
            pltpu.VMEM((OWN, HOLD, 128), f32),
            square_table,
            mailbox,
            mailbox,
            mailbox,
            mailbox,
            pltpu.VMEM((2, 16, 128), f32),
            pltpu.VMEM((2, 16, 128), f32),
            square_table,
            square_table,
            square_table,
            square_table,
            square_table,
            column,
            column,
            column,
            column,
            pltpu.VMEM((SLOTS, 128), bf16),
            pltpu.VMEM((SLOTS, 128), bf16),
            column,
            pltpu.VMEM((2, GROUP, 128), f32),
            pltpu.VMEM((2, GROUP, 128), f32),
            pltpu.VMEM((2, HALF, 128), f32),
            pltpu.VMEM((2, HALF, 128), f32),
            dma,
            dma,
            dma,
            dma,
            dma,
            dma,
            dma((2,)),
            dma((2,)),
            dma((4,)),
            dma((4,)),
        ],
        compiler_params=pltpu.CompilerParams(
            collective_id=0, has_side_effects=True, vmem_limit_bytes=48 << 20
        ),
    )(spectrum, sea_mask, own_speed, slot_speed, owner.astype(f32), coupling)


def solution(mesh):
    return jax.shard_map(
        body,
        mesh=mesh,
        in_specs=(P("wide", "slab", None), P("slab", None), P(), P(), P()),
        out_specs=P("wide", "slab", None),
        check_vma=False,
    )
```

time: 170 us -> 112 us (0.66)
  starting transfers between devices: 20.8 us -> 0 us
  local copies, waits for them, and re-layouts: 24.4 us -> 5.68 us
  waiting for transfers between devices: 17.9 us -> 0 us
  Pallas kernels: 93.4 us -> 100 us
  matrix products: 4.61 us -> 0 us
  other arithmetic: 7.9 us -> 4.84 us
    ppermute x4 -> x0, starting transfers between devices: 20.8 us -> none  [the longest x2 16.9 us: with_halo(): lax.ppermute(first, axis, [(b, a) for a, b in up])]
    ppermute x4 -> x0, waiting for transfers between devices: 17.9 us -> none  [the longest x2 12.8 us: with_halo(): lax.ppermute(last, axis, up)]
    gather x2 -> x0, local copies, waits for them, and re-layouts: 14.4 us -> none  [the longest x1 9.3 us: body(): jnp.take(jnp.take(coupling, slot_owner, axis=0), slot_owner, axis=1)]
    pallas_call x2 -> x1, Pallas kernels: 93.4 us -> 100 us  [body(): pl.pallas_call(kernel, out_shape=jax.ShapeDtypeStruct((OWN, ROWS, 128), f...]
    select_n x1 -> x0, local copies, waits for them, and re-layouts: 5.21 us -> none  [body(): jnp.take(coupling, slot_owner, axis=0)]
    dot_general x4 -> x0, matrix products: 4.61 us -> none  [the longest x2 2.55 us: interact(): jnp.dot(slot_table, rounded, preferred_element_type=jnp.float32)]
    select_n x2 -> x0, other arithmetic: 3.68 us -> none  [the longest x1 3.66 us: body(): jnp.take(coupling, slot_owner, axis=0)]
    unnamed x11 -> x7, local copies, waits for them, and re-layouts: 1.15 us -> 4.46 us
  transfers between devices with their start and end apart: 4 -> 0, of which waited for: 2 -> 0; matrix products, arithmetic and copies ran while one was open for 15% -> 0% of each run, Pallas kernels for 0% -> 0%
where the time goes in v2:
time: 112 us; the launch traced here: 111 us
  Pallas kernels  100 us (89%)
  local copies, waits for them, and re-layouts  5.68 us (5%)
  other arithmetic  4.84 us (4%)
    pallas_call x1, Pallas kernels, body(): pl.pallas_call(kernel, out_shape=jax.ShapeDtypeStruct((OWN, ROWS, 128), f...  100 us
    unnamed x7, local copies, waits for them, and re-layouts  4.46 us

profile of v2, /device:TPU:1, one launch (start us, length us, event | category | flops | bytes accessed | tf_op | source)
XLA Modules:
  0.0 110.8 jit_solution(4309357014017670157)
XLA Ops:
  0.0 0.8 and_select_fusion.1
  0.8 0.8 select_reduce_fusion.1
  1.6 0.8 negate_maximum_fusion
  2.5 0.1 concatenate.6.own_speed
  2.6 0.7 sign_compare_fusion
  3.3 0.2 ne.51
  3.5 0.1 copy.10
  3.6 0.8 fusion.6
  4.4 0.2 convert_element_type.16
  4.6 0.1 copy.13
  4.7 0.2 rem.36
  4.9 0.1 copy.11
  4.9 0.2 div.20
  5.2 0.1 copy.12
  5.3 0.8 select_reduce_fusion
  6.0 0.1 cosine_multiply_fusion
  6.1 0.0 copy-start
  6.1 1.7 %copy-done = bf16[1152,1152]{1,0:T(8,128)(2,1)S(1)} copy-done((bf16[1152,1152]{1,0:T(8,128)(2,1)S(1)}, bf16[1152,1152]{1,0:T(8,128)(2,1)}, u32[]{:S(2)}) %copy-start) | copy-done | bytes 2654232
  7.9 0.0 copy-start.1
  7.9 1.1 copy-done.1
  8.9 0.0 copy-start.2
  8.9 0.8 copy-done.2
  9.8 100.3 %shard_map.55 = f32[9,128,128]{2,1,0:T(8,128)S(1)} custom-call(f32[9,128,128]{2,1,0:T(8,128)S(1)} %copy-done.1, s32[128,128]{1,0:T(8,128)S(1)} %copy-done.2, f32[45]{0:T(128)S(1)} %concatenate.6.own_speed, f32[18,128]{1,0:T(8,128)S(1)} %pad_maximum_fusion.slot_speed, f32[9,128]{1,0:T(8,128)S(1)} %bitcast.25, bf16[1152,1152]{1,0:T(8,128)(2,1)S(1)} %copy-done), custom_call_target="tpu_custom_call" | custom-call | tf_op jit(solution)/shard_map/pallas_call | solution.py:430
  110.0 0.8 copy.15
  (3 shorter events, 0.1 us)
Async XLA Ops:
  6.1 1.8 %copy-start = (bf16[1152,1152]{1,0:T(8,128)(2,1)S(1)}, bf16[1152,1152]{1,0:T(8,128)(2,1)}, u32[]{:S(2)}) copy-start(bf16[1152,1152]{1,0:T(8,128)(2,1)} %coupling.1) | copy-start | bytes 7962628
  7.9 1.1 copy-start.1
  8.9 0.8 copy-start.2

commit v3 on v2

--- a/solution.py
+++ b/solution.py
@@ -8,6 +8,7 @@
 from jax.sharding import PartitionSpec as P
 
 ND = 36
+NF = 32
 WIDE = 128
 OWN = 9
 PAD = 16
@@ -18,6 +19,8 @@
 TILE = 16
 GROUP = 144
 HALF = 72
+EARLY = 32
+FIRST = 2
 MESH = pl.DeviceIdType.MESH
 
 time_step = 0.5
@@ -59,12 +62,18 @@
 
 def kernel(
     spectrum,
-    sea_mask,
-    own_speed,
-    slot_speed,
-    owner,
+    sea_hbm,
+    courant_hbm,
+    owner_hbm,
     coupling,
     out,
+    sea_mask,
+    courant,
+    owner_scalar,
+    owner_rows,
+    owner,
+    own_speed,
+    natural,
     plane,
     table_in,
     outbox,
@@ -90,6 +99,8 @@
     col_out,
     col_in,
     load_sem,
+    sea_sem,
+    small_sem,
     table_sem,
     send_sem,
     recv_sem,
@@ -117,6 +128,14 @@
     east_id = {"slab": slab, "wide": device_of(z, (q + 1) % 8)}
     west_id = {"slab": slab, "wide": device_of(z, (q + 7) % 8)}
 
+    small_loads = [
+        pltpu.make_async_copy(owner_hbm, owner_scalar, small_sem.at[0]),
+        pltpu.make_async_copy(courant_hbm, courant, small_sem.at[1]),
+        pltpu.make_async_copy(owner_hbm, owner_rows, small_sem.at[2]),
+    ]
+    sea_load = pltpu.make_async_copy(sea_hbm, sea_mask, sea_sem)
+    for load in (*small_loads, sea_load):
+        load.start()
     loads = pltpu.make_async_copy(spectrum, plane.at[:, pl.ds(TOP, ROWS)], load_sem)
     loads.start()
     table_load = pltpu.make_async_copy(coupling, table_in, table_sem)
@@ -131,30 +150,48 @@
     ):
         pl.semaphore_signal(barrier, inc=1, device_id=there, device_id_type=MESH)
 
-    def greet(step, carry):
+    def greet(step):
         pl.semaphore_signal(
             barrier, inc=1, device_id={"slab": slab, "wide": peer_of(me, step)}, device_id_type=MESH
         )
-        return carry
-
-    lax.fori_loop(1, WIDE, greet, 0)
+
+    greet(WIDE - 1)
+    for load in small_loads:
+        load.wait()
+    row16 = lax.broadcasted_iota(jnp.int32, (16, 128), 0)
+    own_angle = jnp.zeros((16, 128), jnp.float32)
+    own_courant = jnp.zeros((16, 128), jnp.float32)
+    for j in range(OWN):
+        slot = me * OWN + j
+        component = owner_scalar[slot // 128, slot % 128]
+        freq = component // ND
+        angle = (component - freq * ND).astype(jnp.float32) * (2.0 * math.pi / ND)
+        own_angle = jnp.where(row16 == j, angle, own_angle)
+        own_courant = jnp.where(row16 == j, courant[0, freq], own_courant)
+    east, north = own_courant * jnp.cos(own_angle), own_courant * jnp.sin(own_angle)
+    own_speed[0] = 1.0 - jnp.abs(east) - jnp.abs(north)
+    own_speed[1] = jnp.maximum(east, 0.0)
+    own_speed[2] = jnp.maximum(-east, 0.0)
+    own_speed[3] = jnp.maximum(north, 0.0)
+    own_speed[4] = jnp.maximum(-north, 0.0)
 
     lane = lax.broadcasted_iota(jnp.int32, (8, 128), 1)
     block = lane // TILE
 
+    sea_load.wait()
     loads.wait()
     sea = sea_mask[...].astype(jnp.float32)
     for j in range(OWN):
         plane[j, pl.ds(TOP, ROWS), :] = plane[j, pl.ds(TOP, ROWS), :] * sea
         plane[j, pl.ds(TOP - 8, 8), :] = jnp.zeros((8, 128), jnp.float32)
         plane[j, pl.ds(TOP + ROWS, 8), :] = jnp.zeros((8, 128), jnp.float32)
-        rim_out[0, pl.ds(j, 1), :] = own_speed[3 * OWN + j] * plane[j, pl.ds(TOP + ROWS - 1, 1), :]
-        rim_out[1, pl.ds(j, 1), :] = own_speed[4 * OWN + j] * plane[j, pl.ds(TOP, 1), :]
+        rim_out[0, pl.ds(j, 1), :] = own_speed[3, pl.ds(j, 1), :] * plane[j, pl.ds(TOP + ROWS - 1, 1), :]
+        rim_out[1, pl.ds(j, 1), :] = own_speed[4, pl.ds(j, 1), :] * plane[j, pl.ds(TOP, 1), :]
 
     def propagate(j, carry):
-        remain = own_speed[j]
-        east, west = own_speed[OWN + j], own_speed[2 * OWN + j]
-        north, south = own_speed[3 * OWN + j], own_speed[4 * OWN + j]
+        for u in range(14):
+            greet(j * 14 + u + 1)
+        remain, east, west, north, south = [own_speed[u, pl.ds(j, 1), :] for u in range(5)]
         for h in range(2):
             parts = []
             for k in range(8):
@@ -185,6 +222,42 @@
             )
         )
         rims[-1].start()
+    mine = pl.ds(pl.multiple_of(me * PAD, PAD), OWN)
+    my_tile = pl.ds(pl.multiple_of(spot * PAD, PAD), OWN)
+
+    def send(step, carry):
+        peer = peer_of(me, step)
+        py, pz, px = place(peer)
+        row = (pz * 8 + tile_of(py, px)) * PAD
+        pltpu.make_async_remote_copy(
+            src_ref=outbox.at[pl.ds(pl.multiple_of(row, PAD), OWN)],
+            dst_ref=inbox.at[mine],
+            send_sem=send_sem,
+            recv_sem=recv_sem,
+            device_id={"slab": slab, "wide": peer},
+            device_id_type=MESH,
+        ).start()
+        return carry
+
+    def send_inner(step, carry):
+        _, pz, _ = place(peer_of(me, step))
+
+        @pl.when(jnp.logical_and(pz > 0, pz < 15))
+        def _():
+            send(step, 0)
+
+        return carry
+
+    def send_outer(step, carry):
+        _, pz, _ = place(peer_of(me, step))
+
+        @pl.when(jnp.logical_or(pz == 0, pz == 15))
+        def _():
+            send(step, 0)
+
+        return carry
+
+    lax.fori_loop(1, EARLY, send_inner, 0)
     for rim in rims:
         rim.wait()
     lane9 = lax.broadcasted_iota(jnp.int32, (OWN, 128), 1)
@@ -197,32 +270,24 @@
         high = pltpu.roll(above, 112 - TILE * k, 1) if k < 7 else above
         rows = pl.ds((15 * 8 + k) * PAD, OWN)
         outbox[rows, :] = outbox[rows, :] + jnp.where(lane9 >= 112, high, 0.0)
-
-    mine = pl.ds(pl.multiple_of(me * PAD, PAD), OWN)
-    my_tile = pl.ds(pl.multiple_of(spot * PAD, PAD), OWN)
-
-    def send(step, carry):
-        peer = peer_of(me, step)
-        py, pz, px = place(peer)
-        row = (pz * 8 + tile_of(py, px)) * PAD
-        pltpu.make_async_remote_copy(
-            src_ref=outbox.at[pl.ds(pl.multiple_of(row, PAD), OWN)],
-            dst_ref=inbox.at[mine],
-            send_sem=send_sem,
-            recv_sem=recv_sem,
-            device_id={"slab": slab, "wide": peer},
-            device_id_type=MESH,
-        ).start()
-        return carry
-
-    lax.fori_loop(1, WIDE, send, 0)
+    lax.fori_loop(1, EARLY, send_outer, 0)
+    lax.fori_loop(EARLY, WIDE, send, 0)
     pltpu.make_async_copy(outbox.at[my_tile], inbox.at[mine], recv_sem).start()
 
+    owners = owner_rows[...].astype(jnp.float32)
+    band = jnp.floor((owners + 0.5) * (1.0 / ND))
+    angle = (owners - band * ND) * (2.0 * math.pi / ND)
+    speed = jnp.zeros((OWN, 128), jnp.float32)
+    for f in range(NF):
+        speed = jnp.where(band == f, courant[0, f], speed)
+    wide_rows = (owners, speed * jnp.cos(angle), speed * jnp.sin(angle))
+    for wide_form, row_form in zip((owner_wide, east_wide, north_wide), wide_rows):
+        for j in range(OWN):
+            natural[pl.ds(j * 128, 128), :] = jnp.broadcast_to(row_form[j : j + 1], (128, 128)).T
+        for j in range(OWN):
+            wide_form[pl.ds(j * WIDE, WIDE), :] = natural[pl.ds(j, WIDE, stride=OWN), :]
     for j in range(OWN):
-        rows = pl.ds(j * WIDE, WIDE)
-        owner_wide[rows, :] = jnp.broadcast_to(owner[pl.ds(j, 1), :], (128, 128)).T
-        east_wide[rows, :] = jnp.broadcast_to(slot_speed[pl.ds(j, 1), :], (128, 128)).T
-        north_wide[rows, :] = jnp.broadcast_to(slot_speed[pl.ds(OWN + j, 1), :], (128, 128)).T
+        owner[pl.ds(j, 1), :] = owner_wide[pl.ds(j * WIDE, WIDE), :].T[0:1]
 
     lanes = lax.broadcasted_iota(jnp.int32, (128, 128), 1).astype(jnp.float32)
     sublanes = lax.broadcasted_iota(jnp.int32, (128, 128), 0).astype(jnp.float32)
@@ -378,7 +443,26 @@
         ).start()
         return carry
 
-    lax.fori_loop(1, WIDE, send_back, 0)
+    def send_first(step, carry):
+        _, pz, _ = place(peer_of(me, step))
+
+        @pl.when(pz < FIRST)
+        def _():
+            send_back(step, 0)
+
+        return carry
+
+    def send_later(step, carry):
+        _, pz, _ = place(peer_of(me, step))
+
+        @pl.when(pz >= FIRST)
+        def _():
+            send_back(step, 0)
+
+        return carry
+
+    lax.fori_loop(1, WIDE, send_first, 0)
+    lax.fori_loop(1, WIDE, send_later, 0)
     pltpu.make_async_copy(outbox2.at[mine], inbox2.at[my_tile], recv_sem2).start()
     pltpu.make_async_copy(spectrum, spectrum, recv_sem2).wait()
 
@@ -397,32 +481,9 @@
         pltpu.make_async_copy(rest, rest, sem).wait()
 
 
-def velocities(slot_owner, courant):
-    band_count = courant.shape[0]
-    heading = slot_owner % ND
-    freq_band = slot_owner // ND
-    picked = freq_band[..., None] == jnp.arange(band_count, dtype=jnp.int32)
-    wave_speed = jnp.sum(jnp.where(picked, courant, 0.0), axis=-1)
-    wave_angle = heading.astype(jnp.float32) * (2.0 * math.pi / ND)
-    return wave_speed * jnp.cos(wave_angle), wave_speed * jnp.sin(wave_angle)
-
-
 def body(spectrum, sea_mask, courant, slot_owner, coupling):
-    me = lax.axis_index("wide")
-    east, north = velocities(lax.dynamic_slice_in_dim(slot_owner, me * OWN, OWN), courant)
-    own_speed = jnp.concatenate(
-        [
-            1.0 - jnp.abs(east) - jnp.abs(north),
-            jnp.maximum(east, 0.0),
-            jnp.maximum(-east, 0.0),
-            jnp.maximum(north, 0.0),
-            jnp.maximum(-north, 0.0),
-        ]
-    )
-    owner = slot_owner.reshape(WIDE, OWN).T
-    slot_speed = jnp.concatenate(velocities(owner, courant))
     vmem = pl.BlockSpec(memory_space=pltpu.VMEM)
-    anywhere = pl.BlockSpec(memory_space=pl.ANY)
+    anywhere = pl.BlockSpec(memory_space=pltpu.HBM)
     f32, bf16, dma = jnp.float32, jnp.bfloat16, pltpu.SemaphoreType.DMA
     mailbox = pltpu.VMEM((WIDE * PAD, 128), f32)
     square_table = pltpu.VMEM((SLOTS, SLOTS), bf16)
@@ -430,9 +491,16 @@
     return pl.pallas_call(
         kernel,
         out_shape=jax.ShapeDtypeStruct((OWN, ROWS, 128), f32),
-        in_specs=[anywhere, vmem, pl.BlockSpec(memory_space=pltpu.SMEM), vmem, vmem, anywhere],
+        in_specs=[anywhere] * 5,
         out_specs=vmem,
         scratch_shapes=[
+            pltpu.VMEM((ROWS, 128), jnp.int32),
+            pltpu.SMEM((1, NF), f32),
+            pltpu.SMEM((OWN, 128), jnp.int32),
+            pltpu.VMEM((OWN, 128), jnp.int32),
+            pltpu.VMEM((16, 128), f32),
+            pltpu.VMEM((5, 16, 128), f32),
+            column,
             pltpu.VMEM((OWN, HOLD, 128), f32),
             square_table,
             mailbox,
@@ -459,6 +527,8 @@
             pltpu.VMEM((2, HALF, 128), f32),
             dma,
             dma,
+            dma((3,)),
+            dma,
             dma,
             dma,
             dma,
@@ -469,9 +539,9 @@
             dma((4,)),
         ],
         compiler_params=pltpu.CompilerParams(
-            collective_id=0, has_side_effects=True, vmem_limit_bytes=48 << 20
+            collective_id=0, has_side_effects=True, vmem_limit_bytes=60 << 20
         ),
-    )(spectrum, sea_mask, own_speed, slot_speed, owner.astype(f32), coupling)
+    )(spectrum, sea_mask, courant.reshape(1, NF), slot_owner.reshape(OWN, 128), coupling)
 
 
 def solution(mesh):

time: 112 us -> 106 us (0.946)
  the two profiles are of different devices: /device:TPU:1 before, /device:TPU:96 now
where the time goes in v3:
time: 106 us
  Pallas kernels  104 us (98%)
  local copies, waits for them, and re-layouts  1.92 us (2%)
    pallas_call x1, Pallas kernels, body(): pl.pallas_call(kernel, out_shape=jax.ShapeDtypeStruct((OWN, ROWS, 128), f...  104 us

profile of v3, /device:TPU:96, one launch (start us, length us, event | category | flops | bytes accessed | tf_op | source)
XLA Modules:
  0.0 105.8 jit_solution(5485548356298317640)
XLA Ops:
  0.0 103.9 %shard_map.55 = f32[9,128,128]{2,1,0:T(8,128)} custom-call(f32[9,128,128]{2,1,0:T(8,128)} %spectrum.1, s32[128,128]{1,0:T(8,128)} %sea_hbm.1, f32[1,32]{1,0:T(1,128)} %bitcast.3, s32[9,128]{1,0:T(8,128)} %bitcast.2, bf16[1152,1152]{1,0:T(8,128)(2,1)} %coupling.1), custom_call_target="tpu_custom_call" | custom-call | tf_op jit(solution)/shard_map/pallas_call | solution.py:491
  103.9 1.9 %copy.7 = f32[9,128,128]{2,1,0:T(8,128)} copy(f32[9,128,128]{2,1,0:T(8,128)} %shard_map.55) | data formatting | bytes 1179648

commit v4 on v3

--- a/solution.py
+++ b/solution.py
@@ -19,8 +19,8 @@
 TILE = 16
 GROUP = 144
 HALF = 72
-EARLY = 32
-FIRST = 2
+EARLY = 5
+FIRST = 4
 MESH = pl.DeviceIdType.MESH
 
 time_step = 0.5
@@ -39,12 +39,9 @@
     return y * 64 + z * 4 + jnp.where(y == 0, q, 7 - q)
 
 
-def peer_of(me, step):
-    y, z, x = place(me)
-    turn, plane = step % 16, step // 16
-    half = (turn + 1) // 2
-    dz = jnp.where(turn % 2 == 1, half, 16 - half)
-    return ((y + plane // 4) % 2) * 64 + ((z + dz) % 16) * 4 + (x + plane % 4) % 4
+def distance(turn):
+    far = 8 - (turn + 1) // 2
+    return lax.rem(jnp.where(lax.rem(turn, 2) == 1, far, 16 - far), 16)
 
 
 def swap_blocks(parts, block):
@@ -66,7 +63,7 @@
     courant_hbm,
     owner_hbm,
     coupling,
-    out,
+    inbox2,
     sea_mask,
     courant,
     owner_scalar,
@@ -79,7 +76,6 @@
     outbox,
     inbox,
     outbox2,
-    inbox2,
     rim_out,
     rim_in,
     picker,
@@ -116,6 +112,10 @@
     y, z, x = place(me)
     q = tile_of(y, x)
     spot = z * 8 + q
+    places = []
+    for p in range(8):
+        py, px = lax.rem(y + p // 4, 2), lax.rem(x + p % 4, 4)
+        places.append((py * 64 + px, tile_of(py, px)))
     up_slab, down_slab = (slab + 1) % 4, (slab + 3) % 4
     north_id = {
         "slab": jnp.where(z == 15, up_slab, slab),
@@ -150,12 +150,16 @@
     ):
         pl.semaphore_signal(barrier, inc=1, device_id=there, device_id_type=MESH)
 
-    def greet(step):
-        pl.semaphore_signal(
-            barrier, inc=1, device_id={"slab": slab, "wide": peer_of(me, step)}, device_id_type=MESH
-        )
-
-    greet(WIDE - 1)
+    def greet(turn, first=0):
+        pz = lax.rem(z + distance(turn), 16) if first == 0 else z
+        for base, _ in places[first:]:
+            pl.semaphore_signal(
+                barrier, inc=1, device_id={"slab": slab, "wide": base + pz * 4}, device_id_type=MESH
+            )
+
+    for turn in (0, 1, 2, 3, 13, 14):
+        greet(turn)
+    greet(0, 1)
     for load in small_loads:
         load.wait()
     row16 = lax.broadcasted_iota(jnp.int32, (16, 128), 0)
@@ -189,8 +193,7 @@
         rim_out[1, pl.ds(j, 1), :] = own_speed[4, pl.ds(j, 1), :] * plane[j, pl.ds(TOP, 1), :]
 
     def propagate(j, carry):
-        for u in range(14):
-            greet(j * 14 + u + 1)
+        greet(j + 4)
         remain, east, west, north, south = [own_speed[u, pl.ds(j, 1), :] for u in range(5)]
         for h in range(2):
             parts = []
@@ -225,39 +228,40 @@
     mine = pl.ds(pl.multiple_of(me * PAD, PAD), OWN)
     my_tile = pl.ds(pl.multiple_of(spot * PAD, PAD), OWN)
 
-    def send(step, carry):
-        peer = peer_of(me, step)
-        py, pz, px = place(peer)
-        row = (pz * 8 + tile_of(py, px)) * PAD
-        pltpu.make_async_remote_copy(
-            src_ref=outbox.at[pl.ds(pl.multiple_of(row, PAD), OWN)],
-            dst_ref=inbox.at[mine],
-            send_sem=send_sem,
-            recv_sem=recv_sem,
-            device_id={"slab": slab, "wide": peer},
-            device_id_type=MESH,
-        ).start()
-        return carry
-
-    def send_inner(step, carry):
-        _, pz, _ = place(peer_of(me, step))
+    def send(pz, first=0):
+        for base, tile in places[first:]:
+            pltpu.make_async_remote_copy(
+                src_ref=outbox.at[pl.ds(pl.multiple_of((pz * 8 + tile) * PAD, PAD), OWN)],
+                dst_ref=inbox.at[mine],
+                send_sem=send_sem,
+                recv_sem=recv_sem,
+                device_id={"slab": slab, "wide": base + pz * 4},
+                device_id_type=MESH,
+            ).start()
+
+    def send_inner(turn, carry):
+        pz = lax.rem(z + distance(turn), 16)
 
         @pl.when(jnp.logical_and(pz > 0, pz < 15))
         def _():
-            send(step, 0)
-
-        return carry
-
-    def send_outer(step, carry):
-        _, pz, _ = place(peer_of(me, step))
+            send(pz)
+
+        return carry
+
+    def send_outer(turn, carry):
+        pz = lax.rem(z + distance(turn), 16)
 
         @pl.when(jnp.logical_or(pz == 0, pz == 15))
         def _():
-            send(step, 0)
-
-        return carry
-
-    lax.fori_loop(1, EARLY, send_inner, 0)
+            send(pz)
+
+        return carry
+
+    def send_any(turn, carry):
+        send(lax.rem(z + distance(turn), 16))
+        return carry
+
+    lax.fori_loop(0, EARLY, send_inner, 0)
     for rim in rims:
         rim.wait()
     lane9 = lax.broadcasted_iota(jnp.int32, (OWN, 128), 1)
@@ -270,8 +274,9 @@
         high = pltpu.roll(above, 112 - TILE * k, 1) if k < 7 else above
         rows = pl.ds((15 * 8 + k) * PAD, OWN)
         outbox[rows, :] = outbox[rows, :] + jnp.where(lane9 >= 112, high, 0.0)
-    lax.fori_loop(1, EARLY, send_outer, 0)
-    lax.fori_loop(EARLY, WIDE, send, 0)
+    lax.fori_loop(0, EARLY, send_outer, 0)
+    lax.fori_loop(EARLY, 15, send_any, 0)
+    send(z, 1)
     pltpu.make_async_copy(outbox.at[my_tile], inbox.at[mine], recv_sem).start()
 
     owners = owner_rows[...].astype(jnp.float32)
@@ -393,6 +398,19 @@
             )
         )
         edges[-1].start()
+    for b in range(16):
+        rows = pl.ds(b * HALF, HALF)
+        value = energy[rows, :]
+        west = jnp.where(lane_h % TILE == 0, 0.0, pltpu.roll(value, 1, 1))
+        east = jnp.where(lane_h % TILE == TILE - 1, 0.0, pltpu.roll(value, 127, 1))
+        south = jnp.where(lane_h < TILE, 0.0, pltpu.roll(value, TILE, 1))
+        north = jnp.where(lane_h >= 112, 0.0, pltpu.roll(value, 112, 1))
+        e, n = east_wide[rows, :], north_wide[rows, :]
+        result = (1.0 - jnp.abs(e) - jnp.abs(n)) * value + jnp.maximum(e, 0.0) * west
+        result = result + jnp.maximum(-e, 0.0) * east
+        result = result + jnp.maximum(n, 0.0) * south
+        moved[rows, :] = result + jnp.maximum(-n, 0.0) * north
+
     for edge in edges:
         edge.wait()
 
@@ -404,81 +422,94 @@
         g, u = b // 2, b % 2
         rows = pl.ds(b * HALF, HALF)
         packed = pl.ds(u * HALF, HALF)
-        value = energy[rows, :]
-        west = col_in[0]
+        west, east = col_in[0], col_in[1]
         west = pltpu.roll(west, 128 - b, 1) if b else west
-        west = jnp.where(lane_h % TILE == 0, west, pltpu.roll(value, 1, 1))
-        east = col_in[1]
         east = pltpu.roll(east, 15 - b, 1) if b != 15 else east
-        east = jnp.where(lane_h % TILE == TILE - 1, east, pltpu.roll(value, 127, 1))
         south = keep_south * row_in[0, packed, :]
         south = pltpu.roll(south, 128 - TILE * g, 1) if g else south
-        south = jnp.where(lane_h < TILE, south, pltpu.roll(value, TILE, 1))
         north = keep_north * row_in[1, packed, :]
         north = pltpu.roll(north, 112 - TILE * g, 1) if g < 7 else north
-        north = jnp.where(lane_h >= 112, north, pltpu.roll(value, 112, 1))
         e, n = east_wide[rows, :], north_wide[rows, :]
-        result = (1.0 - jnp.abs(e) - jnp.abs(n)) * value + jnp.maximum(e, 0.0) * west
-        result = result + jnp.maximum(-e, 0.0) * east
-        result = result + jnp.maximum(n, 0.0) * south
-        result = result + jnp.maximum(-n, 0.0) * north
+        result = moved[rows, :]
+        result = result + jnp.where(lane_h % TILE == 0, jnp.maximum(e, 0.0) * west, 0.0)
+        result = result + jnp.where(lane_h % TILE == TILE - 1, jnp.maximum(-e, 0.0) * east, 0.0)
+        result = result + jnp.where(lane_h < TILE, jnp.maximum(n, 0.0) * south, 0.0)
+        result = result + jnp.where(lane_h >= 112, jnp.maximum(-n, 0.0) * north, 0.0)
         moved[rows, :] = result
-    for j in range(OWN):
-        rows = pl.ds(j * WIDE, WIDE)
-        value = moved[rows, :]
-        rounded[rows, :] = value.astype(jnp.bfloat16)
-        square[rows, :] = (value * value).astype(jnp.bfloat16)
+        if u:
+            both = pl.ds(g * GROUP, GROUP)
+            result = moved[both, :]
+            rounded[both, :] = result.astype(jnp.bfloat16)
+            square[both, :] = (result * result).astype(jnp.bfloat16)
     for j in range(OWN):
         outbox2[pl.ds(j, WIDE, stride=PAD), :] = interact(pl.ds(j * WIDE, WIDE))
 
-    def send_back(step, carry):
-        peer = peer_of(me, step)
-        pltpu.make_async_remote_copy(
-            src_ref=outbox2.at[pl.ds(pl.multiple_of(peer * PAD, PAD), OWN)],
-            dst_ref=inbox2.at[my_tile],
-            send_sem=send_sem2,
-            recv_sem=recv_sem2,
-            device_id={"slab": slab, "wide": peer},
-            device_id_type=MESH,
-        ).start()
-        return carry
-
-    def send_first(step, carry):
-        _, pz, _ = place(peer_of(me, step))
-
-        @pl.when(pz < FIRST)
-        def _():
-            send_back(step, 0)
-
-        return carry
-
-    def send_later(step, carry):
-        _, pz, _ = place(peer_of(me, step))
-
-        @pl.when(pz >= FIRST)
-        def _():
-            send_back(step, 0)
-
-        return carry
-
-    lax.fori_loop(1, WIDE, send_first, 0)
-    lax.fori_loop(1, WIDE, send_later, 0)
+    def send_back(pz, some):
+        for base, _ in some:
+            peer = base + pz * 4
+            pltpu.make_async_remote_copy(
+                src_ref=outbox2.at[pl.ds(pl.multiple_of(peer * PAD, PAD), OWN)],
+                dst_ref=inbox2.at[my_tile],
+                send_sem=send_sem2,
+                recv_sem=recv_sem2,
+                device_id={"slab": slab, "wide": peer},
+                device_id_type=MESH,
+            ).start()
+
+    def round_of(favoured, others, own_favoured, own_others):
+        def turns(turn, carry):
+            pz = lax.rem(z + distance(turn), 16)
+            if favoured:
+
+                @pl.when(pz < FIRST)
+                def _():
+                    send_back(pz, favoured)
+
+            if others:
+
+                @pl.when(pz >= FIRST)
+                def _():
+                    send_back(pz, others)
+
+            return carry
+
+        lax.fori_loop(0, 15, turns, 0)
+        if own_favoured:
+
+            @pl.when(z < FIRST)
+            def _():
+                send_back(z, own_favoured)
+
+        if own_others:
+
+            @pl.when(z >= FIRST)
+            def _():
+                send_back(z, own_others)
+
+    round_of(places[:4], (), places[1:4], ())
+    round_of(places[4:], places[:4], places[4:], places[1:4])
+    round_of((), places[4:], (), places[4:])
     pltpu.make_async_copy(outbox2.at[mine], inbox2.at[my_tile], recv_sem2).start()
     pltpu.make_async_copy(spectrum, spectrum, recv_sem2).wait()
 
-    def unpack(j, carry):
-        for h in range(2):
-            parts = [inbox2[pl.ds(h * 128 + k * PAD + j, 8, stride=256), :] for k in range(8)]
-            for k, part in enumerate(swap_blocks(parts, block)):
-                out[j, pl.ds(8 * h + k, 8, stride=16), :] = part
-        return carry
-
-    lax.fori_loop(0, OWN, unpack, 0)
     for sem in (send_sem, send_sem2):
         most = plane.at[pl.ds(0, OWN - 1), pl.ds(0, ROWS)]
         pltpu.make_async_copy(most, most, sem).wait()
         rest = plane.at[0, pl.ds(0, ROWS - OWN)]
         pltpu.make_async_copy(rest, rest, sem).wait()
+
+
+def unpack_kernel(results, out):
+    block = lax.broadcasted_iota(jnp.int32, (8, 128), 1) // TILE
+
+    def unpack(j, carry):
+        for h in range(2):
+            parts = [results[pl.ds(h * 128 + k * PAD + j, 8, stride=256), :] for k in range(8)]
+            for k, part in enumerate(swap_blocks(parts, block)):
+                out[j, pl.ds(8 * h + k, 8, stride=16), :] = part
+        return carry
+
+    lax.fori_loop(0, OWN, unpack, 0)
 
 
 def body(spectrum, sea_mask, courant, slot_owner, coupling):
@@ -488,11 +519,11 @@
     mailbox = pltpu.VMEM((WIDE * PAD, 128), f32)
     square_table = pltpu.VMEM((SLOTS, SLOTS), bf16)
     column = pltpu.VMEM((SLOTS, 128), f32)
-    return pl.pallas_call(
+    results = pl.pallas_call(
         kernel,
-        out_shape=jax.ShapeDtypeStruct((OWN, ROWS, 128), f32),
+        out_shape=jax.ShapeDtypeStruct((WIDE * PAD, 128), f32),
         in_specs=[anywhere] * 5,
-        out_specs=vmem,
+        out_specs=anywhere,
         scratch_shapes=[
             pltpu.VMEM((ROWS, 128), jnp.int32),
             pltpu.SMEM((1, NF), f32),
@@ -503,7 +534,6 @@
             column,
             pltpu.VMEM((OWN, HOLD, 128), f32),
             square_table,
-            mailbox,
             mailbox,
             mailbox,
             mailbox,
@@ -542,6 +572,13 @@
             collective_id=0, has_side_effects=True, vmem_limit_bytes=60 << 20
         ),
     )(spectrum, sea_mask, courant.reshape(1, NF), slot_owner.reshape(OWN, 128), coupling)
+    return pl.pallas_call(
+        unpack_kernel,
+        out_shape=jax.ShapeDtypeStruct((OWN, ROWS, 128), f32),
+        in_specs=[vmem],
+        out_specs=vmem,
+        compiler_params=pltpu.CompilerParams(vmem_limit_bytes=16 << 20),
+    )(results)
 
 
 def solution(mesh):

time: 106 us -> 88.3 us (0.83)
  the two profiles are of different devices: /device:TPU:96 before, /device:TPU:1 now
where the time goes in v4:
time: 88.3 us; the launch traced here: 88.2 us
  Pallas kernels  86.9 us (98%)
  local copies, waits for them, and re-layouts  1.22 us (1%)
    pallas_call x1, Pallas kernels, body(): pl.pallas_call(kernel, out_shape=jax.ShapeDtypeStruct((WIDE * PAD, 128),...  83.9 us
    pallas_call x1, Pallas kernels, body(): pl.pallas_call(unpack_kernel, out_shape=jax.ShapeDtypeStruct((OWN, ROWS,...  3.04 us

profile of v4, /device:TPU:1, one launch (start us, length us, event | category | flops | bytes accessed | tf_op | source)
XLA Modules:
  0.0 88.2 jit_solution(4749473299058375505)
XLA Ops:
  0.0 83.9 %shard_map.55.results = f32[2048,128]{1,0:T(8,128)} custom-call(f32[9,128,128]{2,1,0:T(8,128)} %spectrum.1, s32[128,128]{1,0:T(8,128)} %sea_hbm.1, f32[1,32]{1,0:T(1,128)} %bitcast.3, s32[9,128]{1,0:T(8,128)} %bitcast.2, bf16[1152,1152]{1,0:T(8,128)(2,1)} %coupling.1), custom_call_target="tpu_custom_call" | custom-call | tf_op jit(solution)/shard_map/pallas_call | solution.py:522
  83.9 0.0 copy-start
  83.9 1.2 %copy-done = f32[2048,128]{1,0:T(8,128)S(1)} copy-done((f32[2048,128]{1,0:T(8,128)S(1)}, f32[2048,128]{1,0:T(8,128)}, u32[]{:S(2)}) %copy-start) | copy-done | bytes 1048600
  85.1 3.0 %shard_map.56 = f32[9,128,128]{2,1,0:T(8,128)} custom-call(f32[2048,128]{1,0:T(8,128)S(1)} %copy-done), custom_call_target="tpu_custom_call" | custom-call | tf_op jit(solution)/shard_map/pallas_call | solution.py:575
Async XLA Ops:
  83.9 1.2 %copy-start = (f32[2048,128]{1,0:T(8,128)S(1)}, f32[2048,128]{1,0:T(8,128)}, u32[]{:S(2)}) copy-start(f32[2048,128]{1,0:T(8,128)} %shard_map.55.results) | copy-start | bytes 3145732

commit v5 on v4

--- a/solution.py
+++ b/solution.py
@@ -208,7 +208,7 @@
                 outbox[pl.ds(h * 128 + k * PAD + j, 8, stride=256), :] = part
         return carry
 
-    lax.fori_loop(0, OWN, propagate, 0)
+    lax.fori_loop(0, OWN, propagate, 0, unroll=3)
 
     pl.semaphore_wait(barrier, WIDE - 1 + 4)
 
@@ -509,7 +509,7 @@
                 out[j, pl.ds(8 * h + k, 8, stride=16), :] = part
         return carry
 
-    lax.fori_loop(0, OWN, unpack, 0)
+    lax.fori_loop(0, OWN, unpack, 0, unroll=3)
 
 
 def body(spectrum, sea_mask, courant, slot_owner, coupling):

time: 88.3 us -> 86.6 us (0.981)
  Pallas kernels: 86.9 us -> 84.9 us
    pallas_call x1, Pallas kernels: 3.04 us -> 1.77 us  [body(): pl.pallas_call(unpack_kernel, out_shape=jax.ShapeDtypeStruct((OWN, ROWS,...]
where the time goes in v5:
time: 86.6 us; the launch traced here: 86.2 us
  Pallas kernels  84.9 us (98%)
  local copies, waits for them, and re-layouts  1.22 us (1%)
    pallas_call x1, Pallas kernels, body(): pl.pallas_call(kernel, out_shape=jax.ShapeDtypeStruct((WIDE * PAD, 128),...  83.2 us
    pallas_call x1, Pallas kernels, body(): pl.pallas_call(unpack_kernel, out_shape=jax.ShapeDtypeStruct((OWN, ROWS,...  1.77 us

profile of v5, /device:TPU:1, one launch (start us, length us, event | category | flops | bytes accessed | tf_op | source)
XLA Modules:
  0.0 86.2 jit_solution(6228841778833170940)
XLA Ops:
  0.0 83.2 %shard_map.55.results = f32[2048,128]{1,0:T(8,128)} custom-call(f32[9,128,128]{2,1,0:T(8,128)} %spectrum.1, s32[128,128]{1,0:T(8,128)} %sea_hbm.1, f32[1,32]{1,0:T(1,128)} %bitcast.3, s32[9,128]{1,0:T(8,128)} %bitcast.2, bf16[1152,1152]{1,0:T(8,128)(2,1)} %coupling.1), custom_call_target="tpu_custom_call" | custom-call | tf_op jit(solution)/shard_map/pallas_call | solution.py:522
  83.2 0.0 copy-start
  83.2 1.2 %copy-done = f32[2048,128]{1,0:T(8,128)S(1)} copy-done((f32[2048,128]{1,0:T(8,128)S(1)}, f32[2048,128]{1,0:T(8,128)}, u32[]{:S(2)}) %copy-start) | copy-done | bytes 1048600
  84.4 1.8 %shard_map.56 = f32[9,128,128]{2,1,0:T(8,128)} custom-call(f32[2048,128]{1,0:T(8,128)S(1)} %copy-done), custom_call_target="tpu_custom_call" | custom-call | tf_op jit(solution)/shard_map/pallas_call | solution.py:575
Async XLA Ops:
  83.2 1.2 %copy-start = (f32[2048,128]{1,0:T(8,128)S(1)}, f32[2048,128]{1,0:T(8,128)}, u32[]{:S(2)}) copy-start(f32[2048,128]{1,0:T(8,128)} %shard_map.55.results) | copy-start | bytes 3145732

commit v6 on v5

--- a/solution.py
+++ b/solution.py
@@ -20,7 +20,7 @@
 GROUP = 144
 HALF = 72
 EARLY = 5
-FIRST = 4
+FIRST, SECOND = 2, 6
 MESH = pl.DeviceIdType.MESH
 
 time_step = 0.5
@@ -456,39 +456,28 @@
                 device_id_type=MESH,
             ).start()
 
-    def round_of(favoured, others, own_favoured, own_others):
+    def round_of(*tiers):
         def turns(turn, carry):
             pz = lax.rem(z + distance(turn), 16)
-            if favoured:
-
-                @pl.when(pz < FIRST)
-                def _():
-                    send_back(pz, favoured)
-
-            if others:
-
-                @pl.when(pz >= FIRST)
-                def _():
-                    send_back(pz, others)
+            for low, high, some, _ in tiers:
+
+                @pl.when(jnp.logical_and(pz >= low, pz < high))
+                def _(some=some):
+                    send_back(pz, some)
 
             return carry
 
         lax.fori_loop(0, 15, turns, 0)
-        if own_favoured:
-
-            @pl.when(z < FIRST)
-            def _():
-                send_back(z, own_favoured)
-
-        if own_others:
-
-            @pl.when(z >= FIRST)
-            def _():
-                send_back(z, own_others)
-
-    round_of(places[:4], (), places[1:4], ())
-    round_of(places[4:], places[:4], places[4:], places[1:4])
-    round_of((), places[4:], (), places[4:])
+        for low, high, _, some in tiers:
+
+            @pl.when(jnp.logical_and(z >= low, z < high))
+            def _(some=some):
+                send_back(z, some)
+
+    ahead, behind = places[:4], places[4:]
+    round_of((0, FIRST, places, places[1:]), (FIRST, SECOND, ahead, ahead[1:]))
+    round_of((FIRST, SECOND, behind, behind), (SECOND, 16, ahead, ahead[1:]))
+    round_of((SECOND, 16, behind, behind))
     pltpu.make_async_copy(outbox2.at[mine], inbox2.at[my_tile], recv_sem2).start()
     pltpu.make_async_copy(spectrum, spectrum, recv_sem2).wait()
 

time: 86.6 us -> 86.1 us (level)
  the two profiles are of different devices: /device:TPU:1 before, /device:TPU:65 now
where the time goes in v6:
time: 86.1 us; the launch traced here: 85.9 us
  Pallas kernels  84.7 us (98%)
  local copies, waits for them, and re-layouts  1.22 us (1%)
    pallas_call x1, Pallas kernels, body(): pl.pallas_call(kernel, out_shape=jax.ShapeDtypeStruct((WIDE * PAD, 128),...  82.9 us
    pallas_call x1, Pallas kernels, body(): pl.pallas_call(unpack_kernel, out_shape=jax.ShapeDtypeStruct((OWN, ROWS,...  1.77 us

profile of v6, /device:TPU:65, one launch (start us, length us, event | category | flops | bytes accessed | tf_op | source)
XLA Modules:
  0.0 85.9 jit_solution(11691604964637497370)
XLA Ops:
  0.0 82.9 %shard_map.55.results = f32[2048,128]{1,0:T(8,128)} custom-call(f32[9,128,128]{2,1,0:T(8,128)} %spectrum.1, s32[128,128]{1,0:T(8,128)} %sea_hbm.1, f32[1,32]{1,0:T(1,128)} %bitcast.3, s32[9,128]{1,0:T(8,128)} %bitcast.2, bf16[1152,1152]{1,0:T(8,128)(2,1)} %coupling.1), custom_call_target="tpu_custom_call" | custom-call | tf_op jit(solution)/shard_map/pallas_call | solution.py:511
  82.9 0.0 copy-start
  82.9 1.2 %copy-done = f32[2048,128]{1,0:T(8,128)S(1)} copy-done((f32[2048,128]{1,0:T(8,128)S(1)}, f32[2048,128]{1,0:T(8,128)}, u32[]{:S(2)}) %copy-start) | copy-done | bytes 1048600
  84.1 1.8 %shard_map.56 = f32[9,128,128]{2,1,0:T(8,128)} custom-call(f32[2048,128]{1,0:T(8,128)S(1)} %copy-done), custom_call_target="tpu_custom_call" | custom-call | tf_op jit(solution)/shard_map/pallas_call | solution.py:564
Async XLA Ops:
  82.9 1.2 %copy-start = (f32[2048,128]{1,0:T(8,128)S(1)}, f32[2048,128]{1,0:T(8,128)}, u32[]{:S(2)}) copy-start(f32[2048,128]{1,0:T(8,128)} %shard_map.55.results) | copy-start | bytes 3145732

commit v7 on v6

--- a/solution.py
+++ b/solution.py
@@ -20,7 +20,7 @@
 GROUP = 144
 HALF = 72
 EARLY = 5
-FIRST, SECOND = 2, 6
+FIRST, SECOND = 3, 7
 MESH = pl.DeviceIdType.MESH
 
 time_step = 0.5

time: 86.1 us -> 86.3 us (level)
  the two profiles are of different devices: /device:TPU:65 before, /device:TPU:1 now
where the time goes in v7:
time: 86.3 us; the launch traced here: 86.1 us
  Pallas kernels  84.9 us (98%)
  local copies, waits for them, and re-layouts  1.22 us (1%)
    pallas_call x1, Pallas kernels, body(): pl.pallas_call(kernel, out_shape=jax.ShapeDtypeStruct((WIDE * PAD, 128),...  83.1 us
    pallas_call x1, Pallas kernels, body(): pl.pallas_call(unpack_kernel, out_shape=jax.ShapeDtypeStruct((OWN, ROWS,...  1.77 us

profile of v7, /device:TPU:1, one launch (start us, length us, event | category | flops | bytes accessed | tf_op | source)
XLA Modules:
  0.0 86.1 jit_solution(10764557170551071844)
XLA Ops:
  0.0 83.1 %shard_map.55.results = f32[2048,128]{1,0:T(8,128)} custom-call(f32[9,128,128]{2,1,0:T(8,128)} %spectrum.1, s32[128,128]{1,0:T(8,128)} %sea_hbm.1, f32[1,32]{1,0:T(1,128)} %bitcast.3, s32[9,128]{1,0:T(8,128)} %bitcast.2, bf16[1152,1152]{1,0:T(8,128)(2,1)} %coupling.1), custom_call_target="tpu_custom_call" | custom-call | tf_op jit(solution)/shard_map/pallas_call | solution.py:511
  83.1 0.0 copy-start
  83.1 1.2 %copy-done = f32[2048,128]{1,0:T(8,128)S(1)} copy-done((f32[2048,128]{1,0:T(8,128)S(1)}, f32[2048,128]{1,0:T(8,128)}, u32[]{:S(2)}) %copy-start) | copy-done | bytes 1048600
  84.3 1.8 %shard_map.56 = f32[9,128,128]{2,1,0:T(8,128)} custom-call(f32[2048,128]{1,0:T(8,128)S(1)} %copy-done), custom_call_target="tpu_custom_call" | custom-call | tf_op jit(solution)/shard_map/pallas_call | solution.py:564
Async XLA Ops:
  83.1 1.2 %copy-start = (f32[2048,128]{1,0:T(8,128)S(1)}, f32[2048,128]{1,0:T(8,128)}, u32[]{:S(2)}) copy-start(f32[2048,128]{1,0:T(8,128)} %shard_map.55.results) | copy-start | bytes 3145732
